TPU v7x, 32 devices: a whole 2x2x4 slice. The times are simulated.
32 devices in a mesh: dp: 4 (over y, core), ctx: 2 (over x), seq: 4 (over z).
Axes of the slice: x: 2, y: 2, z: 4, core: 2. Of those that a mesh axis runs over, the one named last changes fastest.
Arguments:
- inputs: bfloat16 [5120, 2304], P(('dp', 'ctx', 'seq')), may hold values from -6 to 6
- positions: int32 [5120], P(('dp', 'ctx')), may hold values from 0 to 4959, as said below
- w_query: bfloat16 [2304, 2048], P(('dp', 'ctx')), may hold values from -0.25 to 0.25
- key_weight: bfloat16 [2304, 1024], P(('dp', 'ctx')), may hold values from -0.1875 to 0.1875
- value_weight: bfloat16 [2304, 1024], P(('dp', 'ctx')), may hold values from -0.125 to 0.125
- w_out: bfloat16 [2304, 2048], P(('dp', 'ctx')), may hold values from -0.125 to 0.125
- w_gate: bfloat16 [9216, 2304], P(('dp', 'ctx')), may hold values from -0.125 to 0.125
- w_up: bfloat16 [9216, 2304], P(('dp', 'ctx')), may hold values from -0.125 to 0.125
- w_down: bfloat16 [9216, 2304], P(('dp', 'ctx')), may hold values from -0.0625 to 0.0625
- gain_attn_in: float32 [2304], replicated, may hold values from -0.75 to 0.75
- gain_attn_out: float32 [2304], replicated, may hold values from -0.75 to 0.75
- gain_ffn_in: float32 [2304], replicated, may hold values from -0.75 to 0.75
- gain_ffn_out: float32 [2304], replicated, may hold values from -0.75 to 0.75
- cotangent: bfloat16 [5120, 2304], P(('dp', 'ctx', 'seq')), may hold values from -6 to 6
Outputs:
- output: float32 [5120, 2304], P(('dp', 'ctx', 'seq'))
- grad_inputs: float32 [5120, 2304], P(('dp', 'ctx', 'seq'))
- grad_w_query: float32 [2304, 2048], P(('dp', 'ctx'))
- grad_w_key: float32 [2304, 1024], P(('dp', 'ctx'))
- grad_w_value: float32 [2304, 1024], P(('dp', 'ctx'))
- grad_w_out: float32 [2304, 2048], P(('dp', 'ctx'))
- grad_w_gate: float32 [9216, 2304], P(('dp', 'ctx'))
- grad_w_up: float32 [9216, 2304], P(('dp', 'ctx'))
- grad_w_down: float32 [9216, 2304], P(('dp', 'ctx'))
- grad_gain_attn_in: float32 [2304], replicated
- grad_gain_attn_out: float32 [2304], replicated
- grad_gain_ffn_in: float32 [2304], replicated
- grad_gain_ffn_out: float32 [2304], replicated
Inputs may be any that keep to these rules, and one draw needn't show every extreme that they name: `positions`: positions count from 0 within each packed document. One document has exactly 4960 tokens and reaches from the first device to the last; the documents before it lie within the first 160 tokens and those after it within the last 160 tokens, in one or more short documents of varying lengths.
All inputs are finite; a program needn't handle non-finite values.
Results may differ from a plain program's by a relative error of at most 0.025.
Values may be sent and summed in bfloat16 or wider, within the bound.
A program may use at most 704 MiB of HBM per device.

v0:
```python
import math

import jax
import jax.numpy as jnp
from jax import lax
from jax.sharding import PartitionSpec as P

HEAD_SIZE = 256
WINDOW = 4096


NORM_EPS = 1e-06
SOFT_CAP = 50.0


def passed_along(array, axis, by):
    devices = lax.axis_size(axis)
    pairs = [(i, i + by) for i in range(devices) if 0 <= i + by < devices]
    return lax.ppermute(array, axis, pairs)


def normed(values, gain_vec):
    return (
        values
        * lax.rsqrt(jnp.mean(values * values, axis=-1, keepdims=True) + NORM_EPS)
        * (1.0 + gain_vec)
    )


def gelu_tanh(values):
    return jax.nn.gelu(values, approximate=True)


def angles(pos_rows, head_dim):
    frequency = jnp.exp(
        jnp.arange(head_dim // 2, dtype=jnp.float32) * (-2.0 * math.log(10000.0) / head_dim)
    )
    turned = pos_rows.astype(jnp.float32)[:, None] * frequency[None, :]
    return (jnp.cos(turned)[:, None, :], jnp.sin(turned)[:, None, :])


def rotate(values, cos_part, sin_part):
    half_dim = values.shape[-1] // 2
    first_half = values[..., :half_dim]
    second_half = values[..., half_dim:]
    return jnp.concatenate(
        [
            first_half * cos_part - second_half * sin_part,
            second_half * cos_part + first_half * sin_part,
        ],
        axis=-1,
    )


def rotate_back(values, cos_part, sin_part):
    half_dim = values.shape[-1] // 2
    first_half = values[..., :half_dim]
    second_half = values[..., half_dim:]
    return jnp.concatenate(
        [
            first_half * cos_part + second_half * sin_part,
            second_half * cos_part - first_half * sin_part,
        ],
        axis=-1,
    )


def dot_last(left_rows, right_rows):
    return lax.dot_general(
        left_rows, right_rows, (((1,), (1,)), ((), ())), preferred_element_type=jnp.float32
    )


def dot_first(left_rows, right_rows):
    return lax.dot_general(
        left_rows, right_rows, (((0,), (0,)), ((), ())), preferred_element_type=jnp.float32
    )


def outer_rows(left_rows, right_rows):
    return dot_first(left_rows, right_rows)


def per_device(
    inputs,
    positions,
    w_query,
    key_weight,
    value_weight,
    w_out,
    w_gate,
    w_up,
    w_down,
    gain_attn_in,
    gain_attn_out,
    gain_ffn_in,
    gain_ffn_out,
    cotangent,
):
    tok_rows, model_width = inputs.shape
    seq_count = lax.axis_size("seq")
    cycle_count = lax.axis_size(("dp", "ctx"))
    cycle_index = lax.axis_index(("dp", "ctx"))
    block_rows = tok_rows * seq_count
    q_width = w_query.shape[1]
    kv_width = key_weight.shape[1]
    q_heads = q_width // HEAD_SIZE
    kv_heads = kv_width // HEAD_SIZE
    grouping_factor = q_heads // kv_heads
    local_kv = kv_heads // seq_count
    local_q = q_heads // seq_count
    back_blocks = min((WINDOW - 2 + block_rows) // block_rows, cycle_count - 1)
    score_scale = HEAD_SIZE ** (-0.5)
    own_positions = lax.dynamic_slice_in_dim(positions, lax.axis_index("seq") * tok_rows, tok_rows)
    cos_part, sin_part = angles(own_positions, HEAD_SIZE)
    residual = inputs.astype(jnp.float32)
    attention_input = normed(residual, gain_attn_in).astype(jnp.bfloat16)
    pieces = (
        lax.all_gather(w_query, ("dp", "ctx"), axis=0, tiled=True),
        lax.all_gather(key_weight, ("dp", "ctx"), axis=0, tiled=True),
        lax.all_gather(value_weight, ("dp", "ctx"), axis=0, tiled=True),
        lax.all_gather(w_out, ("dp", "ctx"), axis=0, tiled=True),
    )
    q_pre = jnp.dot(attention_input, pieces[0], preferred_element_type=jnp.float32)
    key_before_rotary = jnp.dot(attention_input, pieces[1], preferred_element_type=jnp.float32)
    value_acc = jnp.dot(attention_input, pieces[2], preferred_element_type=jnp.float32)
    full_query = pieces[0]
    full_key = pieces[1]
    full_value = pieces[2]
    full_out = pieces[3]
    query_tok = (
        rotate(q_pre.reshape(tok_rows, q_heads, HEAD_SIZE), cos_part, sin_part)
        .reshape(tok_rows, q_width)
        .astype(jnp.bfloat16)
    )
    key_tok = (
        rotate(key_before_rotary.reshape(tok_rows, kv_heads, HEAD_SIZE), cos_part, sin_part)
        .reshape(tok_rows, kv_width)
        .astype(jnp.bfloat16)
    )
    value_tok = value_acc.astype(jnp.bfloat16)
    query_heads, key_heads, value_heads = (
        lax.all_to_all(query_tok, "seq", split_axis=1, concat_axis=0, tiled=True),
        lax.all_to_all(key_tok, "seq", split_axis=1, concat_axis=0, tiled=True),
        lax.all_to_all(value_tok, "seq", split_axis=1, concat_axis=0, tiled=True),
    )
    kv_pairs = [jnp.stack([key_heads, value_heads])]
    for offset in range(back_blocks):
        kv_pairs.append(passed_along(kv_pairs[-1], ("dp", "ctx"), 1))
    query_grouped = query_heads.reshape(block_rows, local_kv, grouping_factor, HEAD_SIZE)
    row_ids = cycle_index * block_rows + jnp.arange(block_rows, dtype=jnp.int32)
    lower_ids = row_ids - jnp.minimum(positions, WINDOW - 1)

    def block_scores(kv_pair, offset):
        key_rows = kv_pair[0].reshape(block_rows, local_kv, HEAD_SIZE)
        raw_scores = jnp.einsum(
            "rkgd,ckd->kgrc", query_grouped, key_rows, preferred_element_type=jnp.float32
        )
        capped = SOFT_CAP * jnp.tanh(raw_scores * score_scale / SOFT_CAP)
        col_ids = (cycle_index - offset) * block_rows + jnp.arange(block_rows, dtype=jnp.int32)
        allowed = (col_ids[None, :] <= row_ids[:, None]) & (col_ids[None, :] >= lower_ids[:, None])
        return (capped, allowed)

    capped, allowed = block_scores(kv_pairs[0], 0)
    row_top = jnp.max(jnp.where(allowed, capped, -1e30), axis=-1)
    running_sum = jnp.sum(jnp.where(allowed, jnp.exp(capped - row_top[..., None]), 0.0), axis=-1)
    for offset in range(1, back_blocks + 1):
        capped, allowed = block_scores(kv_pairs[offset], offset)
        new_top = jnp.maximum(row_top, jnp.max(jnp.where(allowed, capped, -1e30), axis=-1))
        running_sum = running_sum * jnp.exp(row_top - new_top) + jnp.sum(
            jnp.where(allowed, jnp.exp(capped - new_top[..., None]), 0.0), axis=-1
        )
        row_top = new_top
    log_total = row_top + jnp.log(running_sum)
    mixture = jnp.zeros((block_rows, local_kv, grouping_factor, HEAD_SIZE), jnp.float32)
    for offset in range(back_blocks + 1):
        capped, allowed = block_scores(kv_pairs[offset], offset)
        probs_low = jnp.where(allowed, jnp.exp(capped - log_total[..., None]), 0.0).astype(
            jnp.bfloat16
        )
        value_rows = kv_pairs[offset][1].reshape(block_rows, local_kv, HEAD_SIZE)
        mixture = mixture + jnp.einsum(
            "kgrc,ckd->rkgd", probs_low, value_rows, preferred_element_type=jnp.float32
        )
    attn_f32 = mixture.reshape(block_rows, local_q * HEAD_SIZE)
    out_tok = lax.all_to_all(
        attn_f32.astype(jnp.bfloat16), "seq", split_axis=0, concat_axis=1, tiled=True
    )
    branch = dot_last(out_tok, full_out)
    mid = residual + normed(branch, gain_attn_out)
    ffn_in = normed(mid, gain_ffn_in).astype(jnp.bfloat16)
    pieces = (
        lax.all_gather(w_gate, ("dp", "ctx"), axis=0, tiled=True),
        lax.all_gather(w_up, ("dp", "ctx"), axis=0, tiled=True),
        lax.all_gather(w_down, ("dp", "ctx"), axis=0, tiled=True),
    )
    gate_pre = dot_last(ffn_in, pieces[0])
    up_pre = dot_last(ffn_in, pieces[1])
    hidden = (gelu_tanh(gate_pre) * up_pre).astype(jnp.bfloat16)
    unit_result = (
        jnp.dot(hidden, pieces[2], preferred_element_type=jnp.float32),
        hidden,
        gate_pre,
        up_pre,
    )
    ffn_out = unit_result[0]
    hidden_all = unit_result[1]
    grad_out = cotangent.astype(jnp.float32)
    ffn_norm, pull_ffn = jax.vjp(normed, ffn_out, gain_ffn_out)
    output = mid + ffn_norm
    grad_ffn, grad_gain_ffn_out = pull_ffn(grad_out)
    grad_ffn_low = grad_ffn.astype(jnp.bfloat16)
    pieces = (
        lax.all_gather(w_gate, ("dp", "ctx"), axis=0, tiled=True),
        lax.all_gather(w_up, ("dp", "ctx"), axis=0, tiled=True),
        lax.all_gather(w_down, ("dp", "ctx"), axis=0, tiled=True),
    )
    gate_pre = unit_result[2]
    up_pre = unit_result[3]
    grad_hidden = dot_last(grad_ffn_low, pieces[2])
    activated, gelu_pull = jax.vjp(gelu_tanh, gate_pre)
    grad_gate = gelu_pull(grad_hidden * up_pre)[0].astype(jnp.bfloat16)
    grad_up = (grad_hidden * activated).astype(jnp.bfloat16)
    grad_model = jnp.dot(grad_gate, pieces[0], preferred_element_type=jnp.float32) + jnp.dot(
        grad_up, pieces[1], preferred_element_type=jnp.float32
    )
    mid_norm, pull_mid = jax.vjp(normed, mid, gain_ffn_in)
    grad_mid_part, grad_gain_ffn_in = pull_mid(grad_model)
    grad_mid = grad_out + grad_mid_part
    branch_norm, pull_branch = jax.vjp(normed, branch, gain_attn_out)
    grad_branch, grad_gain_attn_out = pull_branch(grad_mid)
    grad_branch_low = grad_branch.astype(jnp.bfloat16)
    grad_attn_tok = jnp.dot(grad_branch_low, full_out, preferred_element_type=jnp.float32).astype(
        jnp.bfloat16
    )
    grad_attn_heads = lax.all_to_all(grad_attn_tok, "seq", split_axis=1, concat_axis=0, tiled=True)
    grad_grouped = grad_attn_heads.reshape(block_rows, local_kv, grouping_factor, HEAD_SIZE)
    out_grouped = attn_f32.reshape(block_rows, local_kv, grouping_factor, HEAD_SIZE)
    row_delta = jnp.transpose(
        jnp.sum(grad_grouped.astype(jnp.float32) * out_grouped, axis=-1), (1, 2, 0)
    )
    grad_query = jnp.zeros((block_rows, local_kv, grouping_factor, HEAD_SIZE), jnp.float32)
    kv_grads = jnp.zeros((2, block_rows, local_kv * HEAD_SIZE), jnp.float32)
    for offset in range(back_blocks, -1, -1):
        kv_pair = kv_pairs[offset]
        capped, allowed = block_scores(kv_pair, offset)
        probs = jnp.where(allowed, jnp.exp(capped - log_total[..., None]), 0.0)
        key_rows = kv_pair[0].reshape(block_rows, local_kv, HEAD_SIZE)
        value_rows = kv_pair[1].reshape(block_rows, local_kv, HEAD_SIZE)
        grad_value = jnp.einsum(
            "kgrc,rkgd->ckd",
            probs.astype(jnp.bfloat16),
            grad_grouped,
            preferred_element_type=jnp.float32,
        )
        grad_probs = jnp.einsum(
            "rkgd,ckd->kgrc", grad_grouped, value_rows, preferred_element_type=jnp.float32
        )
        cap_ratio = capped / SOFT_CAP
        grad_raw = (
            probs
            * (grad_probs - row_delta[..., None])
            * (1.0 - cap_ratio * cap_ratio)
            * score_scale
        ).astype(jnp.bfloat16)
        grad_query = grad_query + jnp.einsum(
            "kgrc,ckd->rkgd", grad_raw, key_rows, preferred_element_type=jnp.float32
        )
        grad_key = jnp.einsum(
            "kgrc,rkgd->ckd", grad_raw, query_grouped, preferred_element_type=jnp.float32
        )
        grad_term = jnp.stack(
            [
                grad_key.reshape(block_rows, local_kv * HEAD_SIZE),
                grad_value.reshape(block_rows, local_kv * HEAD_SIZE),
            ]
        )
        if offset == back_blocks:
            kv_grads = grad_term
        else:
            kv_grads = (
                passed_along(kv_grads.astype(jnp.bfloat16), ("dp", "ctx"), -1).astype(
                    kv_grads.dtype
                )
                + grad_term
            )
    grad_q_heads = grad_query.reshape(block_rows, local_q * HEAD_SIZE).astype(jnp.bfloat16)
    grad_q_tok, grad_k_tok, grad_v_tok = (
        lax.all_to_all(grad_q_heads, "seq", split_axis=0, concat_axis=1, tiled=True),
        lax.all_to_all(
            kv_grads[0].astype(jnp.bfloat16), "seq", split_axis=0, concat_axis=1, tiled=True
        ),
        lax.all_to_all(
            kv_grads[1].astype(jnp.bfloat16), "seq", split_axis=0, concat_axis=1, tiled=True
        ),
    )
    grad_q_pre = (
        rotate_back(
            grad_q_tok.astype(jnp.float32).reshape(tok_rows, q_heads, HEAD_SIZE), cos_part, sin_part
        )
        .reshape(tok_rows, q_width)
        .astype(jnp.bfloat16)
    )
    grad_k_pre = (
        rotate_back(
            grad_k_tok.astype(jnp.float32).reshape(tok_rows, kv_heads, HEAD_SIZE),
            cos_part,
            sin_part,
        )
        .reshape(tok_rows, kv_width)
        .astype(jnp.bfloat16)
    )
    grad_attn_in = (
        dot_last(grad_q_pre, full_query)
        + dot_last(grad_k_pre, full_key)
        + dot_last(grad_v_tok, full_value)
    )
    in_norm, pull_in = jax.vjp(normed, residual, gain_attn_in)
    grad_res_part, grad_gain_attn_in = pull_in(grad_attn_in)
    grad_inputs = grad_mid + grad_res_part
    qkv_grads = jnp.concatenate([grad_q_pre, grad_k_pre, grad_v_tok], axis=1)
    grad_groups = (
        (attention_input, qkv_grads),
        (grad_branch_low, out_tok),
        (grad_gate, ffn_in),
        (grad_up, ffn_in),
        (hidden_all, grad_ffn_low),
    )
    shares = []
    for left_rows, right_rows in grad_groups:
        shares.append(
            lax.psum_scatter(
                outer_rows(left_rows, right_rows).astype(jnp.bfloat16),
                ("dp", "ctx"),
                scatter_dimension=0,
                tiled=True,
            ).astype(jnp.float32)
        )
    shares = (
        lax.psum(shares[0].astype(jnp.bfloat16), "seq").astype(jnp.float32),
        lax.psum(shares[1].astype(jnp.bfloat16), "seq").astype(jnp.float32),
        lax.psum(shares[2].astype(jnp.bfloat16), "seq").astype(jnp.float32),
        lax.psum(shares[3].astype(jnp.bfloat16), "seq").astype(jnp.float32),
        lax.psum(shares[4].astype(jnp.bfloat16), "seq").astype(jnp.float32),
    )
    gain_grads = lax.psum(
        (grad_gain_attn_in, grad_gain_attn_out, grad_gain_ffn_in, grad_gain_ffn_out),
        ("dp", "ctx", "seq"),
    )
    qkv_share = shares[0]
    return (
        output,
        grad_inputs,
        qkv_share[:, :q_width],
        qkv_share[:, q_width : q_width + kv_width],
        qkv_share[:, q_width + kv_width :],
        shares[1],
        shares[2],
        shares[3],
        shares[4],
        gain_grads[0],
        gain_grads[1],
        gain_grads[2],
        gain_grads[3],
    )


def solution(mesh):
    placed = (
        P(("dp", "ctx", "seq"), None),
        P(("dp", "ctx")),
        P(("dp", "ctx"), None),
        P(("dp", "ctx"), None),
        P(("dp", "ctx"), None),
        P(("dp", "ctx"), None),
        P(("dp", "ctx"), None),
        P(("dp", "ctx"), None),
        P(("dp", "ctx"), None),
        P(),
        P(),
        P(),
        P(),
        P(("dp", "ctx", "seq"), None),
    )
    return jax.shard_map(
        per_device,
        mesh=mesh,
        in_specs=placed,
        out_specs=(
            P(("dp", "ctx", "seq"), None),
            P(("dp", "ctx", "seq"), None),
            P(("dp", "ctx"), None),
            P(("dp", "ctx"), None),
            P(("dp", "ctx"), None),
            P(("dp", "ctx"), None),
            P(("dp", "ctx"), None),
            P(("dp", "ctx"), None),
            P(("dp", "ctx"), None),
            P(),
            P(),
            P(),
            P(),
        ),
        check_vma=False,
    )
```

profile of v0, /device:TPU:0, one launch (start us, length us, event | category | flops | bytes accessed | tf_op | source)
XLA Modules:
  0.0 2778.9 jit_solution(14048033335170551018)
XLA Ops:
  12.9 38.6 %all-gather.8.cloned.1.call-done = bf16[2304,1024]{1,0:T(8,128)(2,1)} async-done(((bf16[288,1024]{1,0:T(8,128)(2,1)}), bf16[2304,1024]{1,0:T(8,128)(2,1)}) %all-gather.8.cloned.1.call-update) | async-done | bytes 4718608 | tf_op jit(solution)/shard_map/all_gather | solution.py:121
  55.6 4.6 all-to-all-start
  60.2 32.2 %all-gather.10.cloned.1.call-done = bf16[2304,1024]{1,0:T(8,128)(2,1)} async-done(((bf16[288,1024]{1,0:T(8,128)(2,1)}), bf16[2304,1024]{1,0:T(8,128)(2,1)}) %all-gather.10.cloned.1.call-update) | async-done | bytes 4718608 | tf_op jit(solution)/shard_map/all_gather | solution.py:120
  96.4 15.1 all_to_all.110
  115.0 17.9 collective-permute-done
  132.8 4.4 collective-permute-start.1
  137.2 28.4 %collective-permute-done.1 = bf16[2,640,256]{2,1,0:T(8,128)(2,1)S(1)} collective-permute-done((bf16[2,640,256]{2,1,0:T(8,128)(2,1)S(1)}, bf16[2,640,256]{2,1,0:T(8,128)(2,1)S(1)}, u32[]{:S(2)}, u32[]{:S(2)}) %collective-permute-start.1) | collective-permute-done | bytes 655392 | tf_op jit(solution)/shard_map/ppermute | solution.py:19
  165.7 5.3 collective-permute-start.2
  171.0 13.2 collective-permute-done.2
  184.1 5.3 collective-permute-start.3
  189.5 21.0 collective-permute-done.3
  210.5 5.2 collective-permute-start.4
  215.7 5.4 fusion.250
  223.3 4.6 all-to-all-start.2
  227.9 16.0 collective-permute-done.4
  243.9 5.2 collective-permute-start.5
  252.9 13.2 collective-permute-done.5
  266.1 5.2 collective-permute-start.6
  287.1 6.0 collective-permute-done.6
  322.1 4.8 all-to-all-start.3
  327.0 14.6 all-to-all-done.3
  341.7 7.0 multiply_reduce_fusion.6
  350.5 117.9 %all-gather.16.cloned.1.call-done = bf16[9216,2304]{1,0:T(8,128)(2,1)} async-done(((bf16[1152,2304]{1,0:T(8,128)(2,1)}), bf16[9216,2304]{1,0:T(8,128)(2,1)}) %all-gather.16.cloned.1.call-update) | async-done | bytes 42467344 | tf_op jit(solution)/shard_map/all_gather | solution.py:193
  468.4 24.9 fusion.260
  493.2 176.3 %all-gather.18.cloned.1.call-done = bf16[9216,2304]{1,0:T(8,128)(2,1)} async-done(((bf16[1152,2304]{1,0:T(8,128)(2,1)}), bf16[9216,2304]{1,0:T(8,128)(2,1)}) %all-gather.18.cloned.1.call-update) | async-done | bytes 42467344 | tf_op jit(solution)/shard_map/all_gather | solution.py:194
  669.5 29.2 %multiply_convert_fusion.1 = (bf16[160,9216]{1,0:T(8,128)(2,1)}, f32[160,9216]{1,0:T(8,128)}) fusion(f32[160,9216]{1,0:T(8,128)} %fusion.260, bf16[160,2304]{1,0:T(8,128)(2,1)S(1)} %multiply_convert_fusion.2, bf16[9216,2304]{1,0:T(8,128)(2,1)} %all-gather.18.cloned.1.call-done), kind=kOutput, calls=%fused_computation.15 | convolution fusion | flops 6809518080 | bytes 57950208 | tf_op jit(solution)/shard_map/dot_general | solution.py:69
  698.7 172.1 %all-gather.20.cloned.1.call-done = bf16[9216,2304]{1,0:T(8,128)(2,1)} async-done(((bf16[1152,2304]{1,0:T(8,128)(2,1)}), bf16[9216,2304]{1,0:T(8,128)(2,1)}) %all-gather.20.cloned.1.call-update) | async-done | bytes 42467344 | tf_op jit(solution)/shard_map/all_gather | solution.py:195
  870.8 19.3 multiply_reduce_fusion.4
  892.6 4.1 fusion.143
  896.7 24.4 multiply_convert_fusion
  921.1 19.0 fusion.261
  940.1 20.8 multiply_reduce_fusion
  965.7 5.7 convolution_convert_fusion.5
  972.4 4.6 all-to-all-start.4
  977.0 5.2 convolution_convert_fusion.4
  982.2 12.5 all-to-all-done.4
  1000.7 4.2 fusion.8
  1058.8 13.8 collective-permute-done.7
  1076.0 15.8 collective-permute-done.8
  1095.4 16.1 collective-permute-done.9
  1114.9 15.3 collective-permute-done.10
  1133.7 14.5 collective-permute-done.11
  1151.6 13.5 collective-permute-done.12
  1168.8 12.5 collective-permute-done.13
  1182.4 4.4 all-to-all-start.7
  1187.6 6.4 all-to-all-done.7
  1194.0 4.1 all-to-all-start.6
  1200.3 5.2 all-to-all-done.6
  1206.7 9.2 convolution_convert_fusion.3
  1217.0 27.5 convolution_convert_fusion.1
  1244.8 20.7 convolution_convert_fusion.2
  1266.6 20.3 convolution_convert_fusion
  1287.2 53.2 %reduce-scatter.6.cloned.1.call-done = bf16[288,4096]{1,0:T(8,128)(2,1)} async-done(((bf16[2304,4096]{1,0:T(8,128)(2,1)}), bf16[288,4096]{1,0:T(8,128)(2,1)}) %reduce-scatter.6.cloned.1.call-update) | async-done | bytes 2359312 | tf_op jit(solution)/shard_map/reduce_scatter | solution.py:332
  1340.4 250.6 %reduce-scatter.12.cloned.1.call-done = bf16[1152,2304]{1,0:T(8,128)(2,1)} async-done(((bf16[9216,2304]{1,0:T(8,128)(2,1)}), bf16[1152,2304]{1,0:T(8,128)(2,1)}) %reduce-scatter.12.cloned.1.call-update) | async-done | bytes 5308432 | tf_op jit(solution)/shard_map/reduce_scatter | solution.py:332
  1591.1 251.2 %reduce-scatter.10.cloned.1.call-done = bf16[1152,2304]{1,0:T(8,128)(2,1)} async-done(((bf16[9216,2304]{1,0:T(8,128)(2,1)}), bf16[1152,2304]{1,0:T(8,128)(2,1)}) %reduce-scatter.10.cloned.1.call-update) | async-done | bytes 5308432 | tf_op jit(solution)/shard_map/reduce_scatter | solution.py:332
  1842.3 250.6 %reduce-scatter.14.cloned.1.call-done = bf16[1152,2304]{1,0:T(8,128)(2,1)} async-done(((bf16[9216,2304]{1,0:T(8,128)(2,1)}), bf16[1152,2304]{1,0:T(8,128)(2,1)}) %reduce-scatter.14.cloned.1.call-update) | async-done | bytes 5308432 | tf_op jit(solution)/shard_map/reduce_scatter | solution.py:332
  2093.0 6.9 fusion.262
  2099.9 4.5 convolution_add_fusion.1
  2104.5 5.5 fusion.140
  2110.0 44.5 %all-reduce = (f32[2304]{0:T(1024)}, f32[2304]{0:T(1024)}, f32[2304]{0:T(1024)}, f32[2304]{0:T(1024)}) all-reduce(f32[2304]{0:T(1024)S(1)} %get-tuple-element.19, f32[2304]{0:T(1024)S(1)} %copy-done.91, f32[2304]{0:T(1024)S(1)} %copy-done.96, f32[2304]{0:T(1024)S(1)} %copy-done.90), channel_id=1, replica_groups=mesh['dp'=4,'ctx'=2,'seq'=4] {'dp','ctx','seq'}, use_global_device_ids=true, to_apply=%region_36.37 | all-reduce | flops 9216 | bytes 73728 | tf_op jit(solution)/shard_map/psum | solution.py:346
  2157.3 592.5 %all-reduce.4.cloned.1.call-done = (bf16[288,4096]{1,0:T(8,128)(2,1)}, bf16[288,2048]{1,0:T(8,128)(2,1)}, bf16[1152,2304]{1,0:T(8,128)(2,1)}, bf16[1152,2304]{1,0:T(8,128)(2,1)}, bf16[1152,2304]{1,0:T(8,128)(2,1)}) async-done(((bf16[288,4096]{1,0:T(8,128)(2,1)}, bf16[288,2048]{1,0:T(8,128)(2,1)}, bf16[1152,2304]{1,0:T(8,128)(2,1)}, bf16[1152,2304]{1,0:T(8,128)(2,1)}, bf16[1152,2304]{1,0:T(8,128)(2,1)}), ...) | async-done | bytes 19464208 | tf_op jit(solution)/shard_map/psum | solution.py:340
  2756.4 5.7 convert_element_type.304
  2762.0 4.9 convert_element_type.306
  2767.0 4.9 convert_element_type.308
  (397 shorter events, 174.8 us)
Async XLA Ops:
  7.2 44.4 %all-gather.8.cloned.1.call-start = ((), (), s32[]{:S(2)}) async-start(), calls=%async_computation.13 | async-start | bytes 5308416 | tf_op jit(solution)/shard_map/all_gather | solution.py:121
  7.9 84.5 %all-gather.10.cloned.1.call-start = ((), (), s32[]{:S(2)}) async-start(), calls=%async_computation.14 | async-start | bytes 5308416 | tf_op jit(solution)/shard_map/all_gather | solution.py:120
  8.7 207.0 %all-gather.12.cloned.1.call-start = ((), (), s32[]{:S(2)}) async-start(), calls=%async_computation.15 | async-start | bytes 10616832 | tf_op jit(solution)/shard_map/all_gather | solution.py:119
  9.4 332.3 %all-gather.14.cloned.1.call-start = ((), (), s32[]{:S(2)}) async-start(), calls=%async_computation.16 | async-start | bytes 10616832 | tf_op jit(solution)/shard_map/all_gather | solution.py:122
  10.0 458.4 %all-gather.16.cloned.1.call-start = ((), (), s32[]{:S(2)}) async-start(), calls=%async_computation.17 | async-start | bytes 47775744 | tf_op jit(solution)/shard_map/all_gather | solution.py:193
  10.6 658.9 %all-gather.18.cloned.1.call-start = ((), (), s32[]{:S(2)}) async-start(), calls=%async_computation.18 | async-start | bytes 47775744 | tf_op jit(solution)/shard_map/all_gather | solution.py:194
  11.2 859.6 %all-gather.20.cloned.1.call-start = ((), (), s32[]{:S(2)}) async-start(), calls=%async_computation.19 | async-start | bytes 47775744 | tf_op jit(solution)/shard_map/all_gather | solution.py:195
  12.5 43.1 %copy-start.97 = (f32[160]{0:T(256)}, f32[160]{0:T(256)S(1)}, u32[]{:S(2)}) copy-start(f32[160]{0:T(256)S(1)} %fusion.146) | copy-start | bytes 1924
  12.5 203.2 %copy-start.88 = (f32[160]{0:T(256)}, f32[160]{0:T(256)S(1)}, u32[]{:S(2)}) copy-start(f32[160]{0:T(256)S(1)} %fusion.227) | copy-start | bytes 1924
  12.5 203.2 %copy-start.80 = (f32[2304]{0:T(1024)}, f32[2304]{0:T(1024)S(1)}, u32[]{:S(2)}) copy-start(f32[2304]{0:T(1024)S(1)} %broadcast_add_fusion.3) | copy-start | bytes 27652
  12.9 208.7 %copy-start.50 = (f32[160,128]{1,0:T(8,128)}, f32[160,128]{1,0:T(8,128)S(1)}, u32[]{:S(2)}) copy-start(f32[160,128]{1,0:T(8,128)S(1)} %get-tuple-element.66) | copy-start | bytes 245764
  12.9 208.7 %copy-start.52 = (f32[160,128]{1,0:T(8,128)}, f32[160,128]{1,0:T(8,128)S(1)}, u32[]{:S(2)}) copy-start(f32[160,128]{1,0:T(8,128)S(1)} %get-tuple-element.67) | copy-start | bytes 245764
  55.6 40.7 %all-to-all-start = ((bf16[160,4,256]{2,0,1:T(8,128)(2,1)}), bf16[160,4,256]{2,0,1:T(8,128)(2,1)S(1)}, u32[]{:S(2)}, u32[]{:S(2)}) async-start(bf16[160,4,256]{2,0,1:T(8,128)(2,1)} %bitcast.817), calls=%async_computation | async-start | bytes 655360 | tf_op jit(solution)/shard_map/all_to_all | solution.py:145
  96.3 207.2 %copy-start.76 = (bf16[160,4,256]{2,0,1:T(8,128)(2,1)}, bf16[160,4,256]{2,0,1:T(8,128)(2,1)S(1)}, u32[]{:S(2)}) copy-start(bf16[160,4,256]{2,0,1:T(8,128)(2,1)S(1)} %all-to-all-done) | copy-start | bytes 983044
  111.5 161.2 %copy-start.47 = (bf16[160,4,256]{2,0,1:T(8,128)(2,1)}, bf16[160,4,256]{2,0,1:T(8,128)(2,1)S(1)}, u32[]{:S(2)}) copy-start(bf16[160,4,256]{2,0,1:T(8,128)(2,1)S(1)} %all_to_all.110) | copy-start | bytes 983044
  111.5 21.3 collective-permute-start
  132.8 88.3 %copy-start.82 = (bf16[2,640,256]{2,1,0:T(8,128)(2,1)}, bf16[2,640,256]{2,1,0:T(8,128)(2,1)S(1)}, u32[]{:S(2)}) copy-start(bf16[2,640,256]{2,1,0:T(8,128)(2,1)S(1)} %collective-permute-done) | copy-start | bytes 1966084
  132.8 32.9 %collective-permute-start.1 = (bf16[2,640,256]{2,1,0:T(8,128)(2,1)S(1)}, bf16[2,640,256]{2,1,0:T(8,128)(2,1)S(1)}, u32[]{:S(2)}, u32[]{:S(2)}) collective-permute-start(bf16[2,640,256]{2,1,0:T(8,128)(2,1)S(1)} %collective-permute-done), channel_id=1, source_target_pairs={{0,4},{4,8},{8,12},{12,16},{16,20},{20,24},{24,28},{1,5},{5,9},{9,... | collective-permute-start | bytes 1966088 | tf_op jit(solution)/shard_map/ppermute | solution.py:19
  165.7 55.4 %copy-start.85 = (bf16[2,640,256]{2,1,0:T(8,128)(2,1)}, bf16[2,640,256]{2,1,0:T(8,128)(2,1)S(1)}, u32[]{:S(2)}) copy-start(bf16[2,640,256]{2,1,0:T(8,128)(2,1)S(1)} %collective-permute-done.1) | copy-start | bytes 1966084
  165.7 18.5 collective-permute-start.2
  184.1 26.3 collective-permute-start.3
  210.5 33.4 %collective-permute-start.4 = (bf16[2,640,256]{2,1,0:T(8,128)(2,1)}, bf16[2,640,256]{2,1,0:T(8,128)(2,1)}, u32[]{:S(2)}, u32[]{:S(2)}) collective-permute-start(bf16[2,640,256]{2,1,0:T(8,128)(2,1)} %collective-permute-done.3), channel_id=1, source_target_pairs={{0,4},{4,8},{8,12},{12,16},{16,20},{20,24},{24,28},{1,5},{5,9},{9,... | collective-permute-start | bytes 1966088 | tf_op jit(solution)/shard_map/ppermute | solution.py:19
  223.3 48.1 %all-to-all-start.2 = ((bf16[160,4,512]{2,0,1:T(8,128)(2,1)}), bf16[160,4,512]{2,0,1:T(8,128)(2,1)S(1)}, u32[]{:S(2)}, u32[]{:S(2)}) async-start(bf16[160,4,512]{2,0,1:T(8,128)(2,1)} %copy.286), calls=%async_computation.2 | async-start | bytes 1310720 | tf_op jit(solution)/shard_map/all_to_all | solution.py:143
  243.9 22.2 collective-permute-start.5
  252.9 50.6 %copy-start.54 = (pred[640,640]{0,1:T(8,128)(4,1)}, pred[640,640]{0,1:T(8,128)(4,1)S(1)}, u32[]{:S(2)}) copy-start(pred[640,640]{0,1:T(8,128)(4,1)S(1)} %get-tuple-element.65) | copy-start | bytes 1228804
  252.9 51.9 %copy-start.56 = (pred[640,640]{0,1:T(8,128)(4,1)}, pred[640,640]{0,1:T(8,128)(4,1)S(1)}, u32[]{:S(2)}) copy-start(pred[640,640]{0,1:T(8,128)(4,1)S(1)} %get-tuple-element.58) | copy-start | bytes 1228804
  266.1 27.1 collective-permute-start.6
  272.7 20.5 copy-start
  273.7 29.8 %copy-start.25 = (f32[640,640,2]{1,0,2:T(8,128)}, f32[640,640,2]{1,0,2:T(8,128)S(1)}, u32[]{:S(2)}) copy-start(f32[640,640,2]{1,0,2:T(8,128)S(1)} %get-tuple-element.81) | copy-start | bytes 9830404
  275.3 29.6 %copy-start.27 = (f32[640,640,2]{1,0,2:T(8,128)}, f32[640,640,2]{1,0,2:T(8,128)S(1)}, u32[]{:S(2)}) copy-start(f32[640,640,2]{1,0,2:T(8,128)S(1)} %get-tuple-element.83) | copy-start | bytes 9830404
  277.4 28.7 %copy-start.30 = (f32[640,640,2]{1,0,2:T(8,128)}, f32[640,640,2]{1,0,2:T(8,128)S(1)}, u32[]{:S(2)}) copy-start(f32[640,640,2]{1,0,2:T(8,128)S(1)} %get-tuple-element.79) | copy-start | bytes 9830404
  280.1 27.3 copy-start.33
  282.5 27.2 copy-start.36
  284.8 27.1 copy-start.39
  287.1 27.0 copy-start.42
  295.2 21.4 copy-start.45
  322.1 19.5 all-to-all-start.3
  350.5 319.0 %copy-start.7 = (bf16[160,2304]{1,0:T(8,128)(2,1)}, bf16[160,2304]{1,0:T(8,128)(2,1)S(1)}, u32[]{:S(2)}) copy-start(bf16[160,2304]{1,0:T(8,128)(2,1)S(1)} %multiply_convert_fusion.2) | copy-start | bytes 2211844
  870.8 19.3 copy-start.10
  972.4 22.3 all-to-all-start.4
  977.0 310.3 %reduce-scatter.8.cloned.1.call-start = ((), (), s32[]{:S(2)}) async-start(), calls=%async_computation.21 | async-start | bytes 10616832 | tf_op jit(solution)/shard_map/reduce_scatter | solution.py:332
  1045.3 137.1 %all-to-all-start.5 = ((bf16[4,160,512]{2,1,0:T(8,128)(2,1)}), bf16[4,160,512]{2,1,0:T(8,128)(2,1)S(1)}, u32[]{:S(2)}, u32[]{:S(2)}) async-start(bf16[4,160,512]{2,1,0:T(8,128)(2,1)} %convert_element_type.276), calls=%async_computation.5 | async-start | bytes 1310720 | tf_op jit(solution)/shard_map/all_to_all | solution.py:289
  1054.7 17.8 collective-permute-start.7
  1072.7 19.2 collective-permute-start.8
  1074.7 18.6 copy-start.18
  1076.0 18.0 copy-start.38
  1092.0 19.4 collective-permute-start.9
  1094.0 18.8 copy-start.16
  1095.3 18.2 copy-start.35
  1095.3 18.2 copy-start.63
  1111.5 18.6 collective-permute-start.10
  1113.6 18.0 copy-start.14
  1130.3 17.8 collective-permute-start.11
  1148.3 16.9 collective-permute-start.12
  1165.3 16.0 collective-permute-start.13
  1182.4 11.7 all-to-all-start.7
  1194.0 11.5 all-to-all-start.6
  1198.2 142.3 %reduce-scatter.6.cloned.1.call-start = ((), (), s32[]{:S(2)}) async-start(), calls=%async_computation.20 | async-start | bytes 21233664 | tf_op jit(solution)/shard_map/reduce_scatter | solution.py:332
  1215.9 375.2 %reduce-scatter.12.cloned.1.call-start = ((), (), s32[]{:S(2)}) async-start(), calls=%async_computation.23 | async-start | bytes 47775744 | tf_op jit(solution)/shard_map/reduce_scatter | solution.py:332
  1244.5 597.8 %reduce-scatter.10.cloned.1.call-start = ((), (), s32[]{:S(2)}) async-start(), calls=%async_computation.22 | async-start | bytes 47775744 | tf_op jit(solution)/shard_map/reduce_scatter | solution.py:332
  1265.5 827.5 %reduce-scatter.14.cloned.1.call-start = ((), (), s32[]{:S(2)}) async-start(), calls=%async_computation.24 | async-start | bytes 47775744 | tf_op jit(solution)/shard_map/reduce_scatter | solution.py:332
  1286.9 1462.9 %all-reduce.4.cloned.1.call-start = ((), (), s32[]{:S(2)}) async-start(), calls=%async_computation.25 | async-start | bytes 38928384 | tf_op jit(solution)/shard_map/psum | solution.py:340
  2104.5 50.0 %copy-start.98 = (f32[160]{0:T(256)S(1)}, f32[160]{0:T(256)}, u32[]{:S(2)}) copy-start(f32[160]{0:T(256)} %copy-done.97) | copy-start | bytes 1924
  2104.5 50.0 %copy-start.6 = (f32[160,2304]{1,0:T(8,128)S(1)}, f32[160,2304]{1,0:T(8,128)}, u32[]{:S(2)}) copy-start(f32[160,2304]{1,0:T(8,128)} %copy-done.5) | copy-start | bytes 4423684
  (78 other events, 451.1 us)
Sparse Core Ops, SparseCore 0:
  9.9 41.6 all-gather.7
  53.4 38.9 all-gather.9
  94.3 78.3 all-gather.11
  174.5 84.8 all-gather.13
  261.1 207.2 all-gather.15
  470.1 199.3 all-gather.17
  671.4 199.3 all-gather.19
  982.3 76.9 reduce-scatter.7
  1216.1 124.3 reduce-scatter.5
  1343.9 247.1 reduce-scatter.11
  1595.1 247.1 reduce-scatter.9
  1845.8 247.1 reduce-scatter.13
  2096.4 653.3 all-reduce.3
where the time goes:
time: 2790 us; the launch traced here: 2780 us
  waiting for transfers between devices  2200 us (79%)
  matrix products  347 us (12%)
  starting transfers between devices  75.5 us (3%)
  blocking collectives  59.6 us (2%)
  other arithmetic  48.5 us (2%)
  local copies, waits for them, and re-layouts  36.1 us (1%)
    reduce_scatter x5, waiting for transfers between devices, per_device(): lax.psum_scatter(outer_rows(left_rows, right_rows).astype(jnp.bfloat16),...  806 us
    psum x1, waiting for transfers between devices, per_device(): lax.psum(shares[0].astype(jnp.bfloat16), 'seq').astype(jnp.float32)  593 us
    ppermute x14, waiting for transfers between devices, passed_along(): return lax.ppermute(array, axis, pairs)  217 us
    all_gather x1, waiting for transfers between devices, per_device(): lax.all_gather(w_up, ('dp', 'ctx'), axis=0, tiled=True)  176 us
    all_gather x1, waiting for transfers between devices, per_device(): lax.all_gather(w_down, ('dp', 'ctx'), axis=0, tiled=True)  172 us
    all_gather x1, waiting for transfers between devices, per_device(): lax.all_gather(w_gate, ('dp', 'ctx'), axis=0, tiled=True)  118 us
    dot_general x7, matrix products, dot_last(): lax.dot_general(left_rows, right_rows, (((1,), (1,)), ((), ())), preferre...  102 us
    dot_general x5, matrix products, dot_first(): lax.dot_general(left_rows, right_rows, (((0,), (0,)), ((), ())), preferre...  82.8 us
  transfers between devices with their start and end apart: 34, of which 28 were waited for; matrix products, arithmetic and copies ran while one was open for 11% of the time, Pallas kernels for 0%

commit v1 on v0

v1 whole, which is shorter than its diff:
```python
import functools
import math

import jax
import jax.numpy as jnp
from jax import lax
from jax.experimental import pallas as pl
from jax.experimental.pallas import tpu as pltpu
from jax.sharding import PartitionSpec as P

HEAD_SIZE = 256
WINDOW = 4096


NORM_EPS = 1e-06
SOFT_CAP = 50.0
UNIT_ROWS = 128
CHUNK_ROWS = 64
SHORT_CHUNK_ROWS = 32
GIVEN_ROWS = 96
EARLY_STEPS = 5
EARLY_UNITS = 2
GELU_SCALE = math.sqrt(2.0 / math.pi)
MESH = pl.DeviceIdType.MESH


def summed(array, axes):
    return lax.psum(array.astype(jnp.bfloat16), axes)


def after(arrays, others):
    return lax.optimization_barrier((tuple(arrays), tuple(others)))[0]


def normed(values, gain_vec):
    return (
        values
        * lax.rsqrt(jnp.mean(values * values, axis=-1, keepdims=True) + NORM_EPS)
        * (1.0 + gain_vec)
    )


def gelu_tanh(values):
    return jax.nn.gelu(values, approximate=True)


def angles(pos_rows, head_dim):
    frequency = jnp.exp(
        jnp.arange(head_dim // 2, dtype=jnp.float32) * (-2.0 * math.log(10000.0) / head_dim)
    )
    turned = pos_rows.astype(jnp.float32)[:, None] * frequency[None, :]
    return (jnp.cos(turned)[:, None, :], jnp.sin(turned)[:, None, :])


def rotate(values, cos_part, sin_part):
    half_dim = values.shape[-1] // 2
    first_half = values[..., :half_dim]
    second_half = values[..., half_dim:]
    return jnp.concatenate(
        [
            first_half * cos_part - second_half * sin_part,
            second_half * cos_part + first_half * sin_part,
        ],
        axis=-1,
    )


def rotate_back(values, cos_part, sin_part):
    half_dim = values.shape[-1] // 2
    first_half = values[..., :half_dim]
    second_half = values[..., half_dim:]
    return jnp.concatenate(
        [
            first_half * cos_part + second_half * sin_part,
            second_half * cos_part - first_half * sin_part,
        ],
        axis=-1,
    )


def dot_last(left_rows, right_rows):
    return lax.dot_general(
        left_rows, right_rows, (((1,), (1,)), ((), ())), preferred_element_type=jnp.float32
    )


def dot_first(left_rows, right_rows):
    return lax.dot_general(
        left_rows, right_rows, (((0,), (0,)), ((), ())), preferred_element_type=jnp.float32
    )


def gathered(array, axes):
    return lax.all_gather(array, axes, axis=0, tiled=True)


def scattered_low(array, axes):
    return lax.psum_scatter(array.astype(jnp.bfloat16), axes, scatter_dimension=0, tiled=True)


def scattered(array, axes):
    return scattered_low(array, axes).astype(jnp.float32)


def greet(partners):
    barrier = pltpu.get_barrier_semaphore()
    for partner in partners:
        pl.semaphore_signal(barrier, inc=1, device_id=partner, device_id_type=MESH)
    pl.semaphore_wait(barrier, len(partners))


class Cube:
    def __init__(self, dp_count, ctx_count):
        self.dp_count, self.ctx_count = dp_count, ctx_count
        count = dp_count * ctx_count
        self.far_bits = [
            1 << at for at in range(count.bit_length() - 1) if (1 << at) != ctx_count
        ]
        self.stages = len(self.far_bits)
        self.chips = 1 << self.stages

    def across(self, bit):
        dp, ctx = lax.axis_index("dp"), lax.axis_index("ctx")
        if bit < self.ctx_count:
            return dp, ctx + bit * (1 - 2 * lax.rem(ctx // bit, 2))
        bit = bit // self.ctx_count
        return dp + bit * (1 - 2 * lax.rem(dp // bit, 2)), ctx

    def device_across(self, bit):
        dp, ctx = self.across(bit)
        return {"dp": dp, "ctx": ctx}

    def sibling(self):
        dp, ctx = self.across(self.ctx_count)
        return {"dp": dp, "ctx": ctx}

    def far(self, stage):
        core = lax.rem(lax.axis_index("dp"), 2)
        dp0, ctx0 = self.across(self.far_bits[stage])
        dp1, ctx1 = self.across(self.far_bits[self.stages - 1 - stage])
        return {"dp": dp0 + core * (dp1 - dp0), "ctx": ctx0 + core * (ctx1 - ctx0)}

    def index(self):
        return lax.axis_index("dp") * self.ctx_count + lax.axis_index("ctx")

    def owner(self, block, half):
        index = self.index()
        core = lax.rem(lax.axis_index("dp"), 2)
        flipped = core + half - 2 * core * half

        def change(bit):
            return bit * (1 - 2 * lax.rem(index // bit, 2))

        owner = index + half * change(self.ctx_count)
        for stage in range(self.stages):
            change0 = change(self.far_bits[stage])
            change1 = change(self.far_bits[self.stages - 1 - stage])
            taken = lax.rem(block // (1 << stage), 2)
            owner = owner + taken * (change0 + flipped * (change1 - change0))
        return owner

    def partners(self):
        return [self.sibling()] + [self.far(stage) for stage in range(self.stages)]

    def greet(self):
        greet(self.partners())

    def stage_of(self, block):
        return block.bit_length() - 1

    def semaphores(self):
        per_block = pltpu.SemaphoreType.DMA((self.chips,))
        per_stage = pltpu.SemaphoreType.DMA((self.chips,))
        return [per_block, per_block, per_stage, per_stage] * 2


def remote(source, target, send_sem, recv_sem, device):
    return pltpu.make_async_remote_copy(
        src_ref=source,
        dst_ref=target,
        send_sem=send_sem,
        recv_sem=recv_sem,
        device_id=device,
        device_id_type=MESH,
    )


def gather_work_scatter(cube, own, whole, part, from_core, from_far, sems, arrived, work, partners=None, beside=None):
    core_send, core_recv, far_send, far_recv, back_send, back_recv, sum_send, sum_recv = sems
    stages, chips = cube.stages, cube.chips
    sibling = cube.sibling()
    fars = [cube.far(stage) for stage in range(stages)]

    def to_core(block):
        return remote(
            whole.at[block, 0], whole.at[block, 1], core_send.at[block], core_recv.at[block], sibling
        )

    def to_far(block, stage):
        at = block + (1 << stage)
        return remote(
            whole.at[block, 0], whole.at[at, 0], far_send.at[at], far_recv.at[at], fars[stage]
        )

    def sum_to_core(block):
        return remote(
            part.at[block, 1], from_core.at[block], back_send.at[block], back_recv.at[block], sibling
        )

    def sum_to_far(block):
        stage = cube.stage_of(block)
        return remote(
            part.at[block, 0], from_far.at[block], sum_send.at[block], sum_recv.at[block], fars[stage]
        )

    def fold(block):
        sum_to_core(block).wait_recv()
        part[block, 0] = (
            part[block, 0].astype(jnp.float32) + from_core[block].astype(jnp.float32)
        ).astype(jnp.bfloat16)
        if stages and block >= chips // 2:
            sum_to_far(block).start()

    def relay():
        for stage in reversed(range(stages)):
            for block in reversed(range(1, 1 << stage)):
                slot = block + (1 << stage)
                sum_to_far(slot).wait_recv()
                part[block, 0] = (
                    part[block, 0].astype(jnp.float32) + from_far[slot].astype(jnp.float32)
                ).astype(jnp.bfloat16)
                if cube.stage_of(block) == stage - 1:
                    sum_to_far(block).start()

    beside = beside or (lambda point: None)
    greet(partners or cube.partners())
    whole[0, 0] = own[...]
    if stages:
        to_far(0, 0).start()
    to_core(0).start()
    for block in [*range(1, chips), 0]:
        if block:
            stage = cube.stage_of(block)
            to_far(block - (1 << stage), stage).wait_recv()
            if block == 1:
                for later in range(1, stages):
                    to_far(0, later).start()
            for later in range(stage + 1, stages):
                to_far(block, later).start()
            to_core(block).start()
            to_core(block).wait_recv()
        if block == 1:
            to_core(0).wait_recv()
        arrived(block)
        if block == chips - 1:
            beside(0)
        if not block and chips > 1:
            fold(chips - 1)
            beside(1)
        between = functools.partial(fold, block - 1) if block > 1 else None
        work(block, between if block else relay)
        sum_to_core(block).start()
    beside(2)
    sum_to_core(0).wait_recv()
    total = part[0, 0].astype(jnp.float32) + from_core[0].astype(jnp.float32)
    for stage in reversed(range(stages)):
        sum_to_far(1 << stage).wait_recv()
        total = total + from_far[1 << stage].astype(jnp.float32)
    for block in range(chips):
        to_core(block).wait_send()
        sum_to_core(block).wait_send()
        if block:
            stage = cube.stage_of(block)
            to_far(block - (1 << stage), stage).wait_send()
            sum_to_far(block).wait_send()
    return total


def tiles_of(width, most):
    tile = max(size for size in range(128, most + 1, 128) if width % size == 0)
    return [pl.ds(first, tile) for first in range(0, width, tile)]


def ffn_forward_kernel(
    cube, own, w_gate, w_up, w_down, out, whole_out, hidden_out, act_out, slope_out,
    whole, gate_rows, up_rows, down_rows, hidden, act, slope, part, from_core, from_far,
    load, save, *sems,
):
    chips = cube.chips
    units, width = gate_rows.shape
    rows = 2 * own.shape[0]
    loads = [
        pltpu.make_async_copy(source, target, load.at[at])
        for at, (source, target) in enumerate(
            [(w_gate, gate_rows), (w_up, up_rows), (w_down, down_rows)]
        )
    ]
    for copy in loads:
        copy.start()

    kept = [(whole, whole_out), (hidden, hidden_out), (act, act_out), (slope, slope_out)]

    def saved(kind, block):
        source, target = kept[kind]
        return pltpu.make_async_copy(source.at[block], target.at[block], save.at[kind, block])

    def arrived(block):
        saved(0, block).start()

    def work(block, between):
        if block == 1:
            loads[0].wait()
            loads[1].wait()
        tokens = whole[block].reshape(rows, width)
        for tile in tiles_of(units, 384):
            gate = dot_last(tokens, gate_rows[tile, :])
            up = dot_last(tokens, up_rows[tile, :])
            square = gate * gate
            bent = jnp.tanh(GELU_SCALE * gate * (1.0 + 0.044715 * square))
            half = 0.5 + 0.5 * bent
            active = gate * half
            steep = half + (0.5 * GELU_SCALE) * gate * (1.0 - bent * bent) * (
                1.0 + (3 * 0.044715) * square
            )
            hidden[block, :, tile] = (active * up).astype(jnp.bfloat16)
            act[block, :, tile] = active.astype(jnp.bfloat16)
            slope[block, :, tile] = (up * steep).astype(jnp.bfloat16)
        if block == 1:
            loads[2].wait()
        units_now = hidden[block]
        for tile in tiles_of(width, 768):
            sums = jnp.dot(units_now, down_rows[:, tile], preferred_element_type=jnp.float32)
            part[block, :, :, tile] = sums.astype(jnp.bfloat16).reshape(2, rows // 2, tile.size)
        for kind in range(1, len(kept)):
            saved(kind, block).start()
        if between:
            between()

    out[...] = gather_work_scatter(
        cube, own, whole, part, from_core, from_far, sems, arrived, work
    )
    for block in range(chips):
        for kind in range(len(kept)):
            saved(kind, block).wait()


def ffn_backward_kernel(
    cube, own, w_gate, w_up, w_down, act_in, slope_in, hidden_in, out, whole_out, gate_out, up_out,
    early_out, whole, gate_rows, up_rows, down_rows, act, slope, part, from_core, from_far,
    load, save, hidden, line_own, from_end, from_middle, line_sems, *sems,
):
    chips = cube.chips
    units, width = gate_rows.shape
    rows = 2 * own.shape[0]
    loads = [
        pltpu.make_async_copy(source, target, load.at[at])
        for at, (source, target) in enumerate(
            [
                (w_down, down_rows),
                (act_in, act),
                (slope_in, slope),
                (w_gate, gate_rows),
                (w_up, up_rows),
                (hidden_in.at[:, :, pl.ds(0, hidden.shape[2])], hidden),
            ]
        )
    ]
    for copy in loads:
        copy.start()

    kept = [(whole, whole_out), (slope, gate_out), (act, up_out)]

    def saved(kind, block):
        source, target = kept[kind]
        return pltpu.make_async_copy(source.at[block], target.at[block], save.at[kind, block])

    def arrived(block):
        saved(0, block).start()

    def work(block, between):
        if block == 1:
            for copy in loads[:3]:
                copy.wait()
        grads = whole[block].reshape(rows, width)
        for tile in tiles_of(units, 384):
            grad_hidden = dot_last(grads, down_rows[tile, :])
            slope[block, :, tile] = (
                grad_hidden * slope[block, :, tile].astype(jnp.float32)
            ).astype(jnp.bfloat16)
            act[block, :, tile] = (grad_hidden * act[block, :, tile].astype(jnp.float32)).astype(
                jnp.bfloat16
            )
        if block == 1:
            for copy in loads[3:]:
                copy.wait()
        if between:
            between()
        grad_gate, grad_up = slope[block], act[block]
        for tile in tiles_of(width, 768):
            sums = jnp.dot(grad_gate, gate_rows[:, tile], preferred_element_type=jnp.float32)
            sums = sums + jnp.dot(grad_up, up_rows[:, tile], preferred_element_type=jnp.float32)
            part[block, :, :, tile] = sums.astype(jnp.bfloat16).reshape(2, rows // 2, tile.size)
        for kind in range(1, len(kept)):
            saved(kind, block).start()

    line = Line()
    job = LineJob(line, line_own, from_end, from_middle, from_end, early_out, line_sems)
    per_unit = job.depth = UNIT_ROWS // line_own.shape[1]

    def beside(point):
        chunks = range(point * per_unit, (point + 1) * per_unit)
        if point < EARLY_UNITS:
            unit_product(hidden, whole, line_own, point)

            @pl.when(line.is_end)
            def _():
                for at in chunks:
                    job.send_end(jnp.int32(at))

        if point:

            @pl.when(jnp.logical_not(line.is_end))
            def _():
                for at in chunks:
                    job.add_middle(jnp.int32(at - per_unit))
                if point == EARLY_UNITS:
                    job.finish_middle(job.count - 1)

    out[...] = gather_work_scatter(
        cube,
        own,
        whole,
        part,
        from_core,
        from_far,
        sems,
        arrived,
        work,
        cube.partners() + [{"seq": lax.rem(line.place + ahead, 4)} for ahead in range(1, 4)],
        beside,
    )

    @pl.when(line.is_end)
    def _():
        job.close_end()

    @pl.when(jnp.logical_not(line.is_end))
    def _():
        job.close_middle()

    for block in range(chips):
        for kind in range(len(kept)):
            saved(kind, block).wait()


def cube_fits(dp_count, ctx_count, tok_rows, units, width):
    count = dp_count * ctx_count
    if count & (count - 1) or dp_count % 2:
        return False
    tokens = count * tok_rows
    held = 2 * (5 * tokens * width // 2 + 3 * units * width + 3 * tokens * units)
    return held <= 48 * 2**20 and tok_rows % 16 == 0


def ffn_call(kernel, cube, collective_id, own, weights, extras, kept, early=()):
    tok_rows, width = own.shape
    units = weights[0].shape[0]
    chips = cube.chips
    rows = 2 * tok_rows
    low = jnp.bfloat16
    unit_block = (chips, rows, units)
    inside = pl.BlockSpec(memory_space=pltpu.VMEM)
    outside = pl.BlockSpec(memory_space=pl.ANY)
    chunks = (EARLY_UNITS * UNIT_ROWS // SHORT_CHUNK_ROWS, SHORT_CHUNK_ROWS, width)
    line_scratch = [
        pltpu.VMEM((chips, rows, EARLY_UNITS * UNIT_ROWS), low),
        pltpu.VMEM(chunks, low),
        pltpu.VMEM(chunks, low),
        pltpu.VMEM(chunks, low),
        pltpu.SemaphoreType.DMA((7, chunks[0])),
    ]
    return pl.pallas_call(
        functools.partial(kernel, cube),
        out_shape=[
            jax.ShapeDtypeStruct((tok_rows, width), jnp.float32),
            jax.ShapeDtypeStruct((chips, 2, tok_rows, width), low),
        ]
        + [jax.ShapeDtypeStruct(unit_block, low)] * kept
        + [jax.ShapeDtypeStruct(chunks, low)] * len(early),
        in_specs=[inside] + [outside] * (3 + len(extras) + len(early)),
        out_specs=[inside] + [outside] * (1 + kept + len(early)),
        scratch_shapes=[pltpu.VMEM((chips, 2, tok_rows, width), low)]
        + [pltpu.VMEM((units, width), low)] * 3
        + [pltpu.VMEM(unit_block, low)] * max(kept, len(extras))
        + [
            pltpu.VMEM((chips, 2, tok_rows, width), low),
            pltpu.VMEM((chips, tok_rows, width), low),
            pltpu.VMEM((chips, tok_rows, width), low),
            pltpu.SemaphoreType.DMA((3 + len(extras) + len(early),)),
            pltpu.SemaphoreType.DMA((1 + kept, chips)),
        ]
        + line_scratch * len(early)
        + cube.semaphores(),
        compiler_params=pltpu.CompilerParams(
            collective_id=collective_id,
            has_side_effects=True,
            vmem_limit_bytes=60 * 2**20,
        ),
        cost_estimate=pl.CostEstimate(
            flops=6 * chips * rows * units * width,
            bytes_accessed=6 * units * width + 6 * chips * rows * units,
            transcendentals=0,
        ),
    )(own, *weights, *extras, *early)


class Line:
    def __init__(self):
        self.place = lax.axis_index("seq")
        self.is_end = (self.place == 0) | (self.place == 3)
        low = self.place // 2
        self.end = {"seq": 3 * low}
        self.middle = {"seq": 1 + low}
        self.other_middle = {"seq": 2 - low}


class LineJob:
    def __init__(self, line, own, from_end, from_middle, total, out, sems):
        self.line = line
        self.own, self.from_end, self.from_middle = own, from_end, from_middle
        self.total, self.out, self.sems = total, out, sems
        self.count = own.shape[0]
        self.before = None
        self.first = 0
        self.depth = 2

    def inward(self, at):
        sems = self.sems
        return remote(
            self.own.at[at], self.from_end.at[at], sems.at[0, at], sems.at[1, at], self.line.middle
        )

    def across(self, at):
        sems = self.sems
        return remote(
            self.own.at[at],
            self.from_middle.at[at],
            sems.at[2, at],
            sems.at[3, at],
            self.line.other_middle,
        )

    def outward(self, at):
        sems = self.sems
        return remote(
            self.total.at[at], self.total.at[at], sems.at[4, at], sems.at[5, at], self.line.end
        )

    def save(self, at):
        return pltpu.make_async_copy(
            self.total.at[at], self.out.at[at + self.first], self.sems.at[6, at]
        )

    def send_end(self, at):
        @pl.when(at >= self.depth)
        def _():
            self.inward(at - self.depth).wait_send()

        self.inward(at).start()

    def add_middle(self, at):
        self.inward(at).wait_recv()
        self.own[at] = (
            self.own[at].astype(jnp.float32) + self.from_end[at].astype(jnp.float32)
        ).astype(jnp.bfloat16)
        self.across(at).start()

        @pl.when(at >= 1)
        def _():
            self.finish_middle(at - 1)

        if self.before:

            @pl.when(at == 0)
            def _():
                self.before.finish_middle(self.before.count - 1)

    def finish_middle(self, at):
        self.across(at).wait_recv()
        self.total[at] = (
            self.own[at].astype(jnp.float32) + self.from_middle[at].astype(jnp.float32)
        ).astype(jnp.bfloat16)
        self.outward(at).start()
        self.save(at).start()

    def each(self, body):
        def step(at, carry):
            body(at)
            return carry

        lax.fori_loop(0, self.count, step, 0)

    def close_end(self):
        def body(at):
            self.outward(at).wait_recv()
            self.save(at).start()

        self.each(body)
        self.each(lambda at: self.save(at).wait())
        for at in range(max(self.count - self.depth, 0), self.count):
            self.inward(at).wait_send()

    def close_middle(self):
        def body(at):
            self.across(at).wait_send()
            self.outward(at).wait_send()
            self.save(at).wait()

        self.each(body)


class Spread:
    def __init__(self, line, block, slots, sems, out=None, shares=(), save=None):
        self.place, self.block, self.slots, self.sems = line.place, block, slots, sems
        self.out, self.shares, self.save = out, shares, save

    def hop(self, way, turn, slot):
        sems = self.sems
        at = 0 if way > 0 else 2
        return remote(
            self.slots.at[slot],
            self.slots.at[slot],
            sems.at[at, turn],
            sems.at[at + 1, turn],
            {"seq": self.place + way},
        )

    def each(self, turn, held, body):
        for way in (1, -1):
            slot = self.place - way * (turn if held else turn + 1)
            near = self.place + way if held else self.place - way
            inside = (slot >= 0) & (slot <= 3) & (near >= 0) & (near <= 3)

            @pl.when(inside)
            def _(way=way, slot=slot):
                body(self.hop(way, turn, slot) if held else self.arrival(way, turn, slot))

    def arrival(self, way, turn, slot):
        at = 0 if way > 0 else 2
        return remote(
            self.slots.at[slot],
            self.slots.at[slot],
            self.sems.at[at, turn],
            self.sems.at[at + 1, turn],
            {"seq": self.place - way},
        )

    def start(self):
        self.slots[self.place] = self.block[...]
        self.each(0, True, lambda copy: copy.start())

    def forward_turn(self, turn):
        self.each(turn - 1, False, lambda copy: copy.wait_recv())
        if turn <= 2:
            self.each(turn, True, lambda copy: copy.start())

    def forward(self):
        self.forward_turn(1)
        self.forward_turn(2)

    def close_sends(self):
        for turn in range(3):
            self.each(turn, True, lambda copy: copy.wait_send())

    def close(self):
        self.forward_turn(3)
        if self.out is None:
            self.close_sends()
            return
        saves, first = [], 0
        for share in self.shares:
            for slot in range(4):
                source = self.slots.at[slot, :, pl.ds(first, share)]
                target = self.out.at[:, pl.ds(4 * first + slot * share, share)]
                saves.append(pltpu.make_async_copy(source, target, self.save.at[len(saves)]))
            first += share
        for save in saves:
            save.start()
        self.close_sends()
        for save in saves:
            save.wait()


class Swap:
    def __init__(self, blocks, landed, send_sems, recv_sems):
        self.blocks, self.landed = blocks, landed
        self.send_sems, self.recv_sems = send_sems, recv_sems
        self.count = blocks.shape[0]
        self.place = lax.axis_index("seq")

    def peer(self, ahead):
        return lax.rem(self.place + ahead, self.count)

    def copy(self, ahead, slot):
        peer = self.peer(ahead)
        return remote(
            self.blocks.at[peer],
            self.landed.at[slot],
            self.send_sems.at[ahead],
            self.recv_sems.at[ahead],
            {"seq": peer},
        )

    def start(self, ahead):
        self.copy(ahead, self.place).start()

    def keep(self):
        self.landed[self.place] = self.blocks[self.place]

    def wait_recv(self):
        for ahead in range(1, self.count):
            self.copy(ahead, self.peer(self.count - ahead)).wait_recv()

    def wait_send(self):
        for ahead in range(1, self.count):
            self.copy(ahead, self.place).wait_send()

    def others(self):
        return [{"seq": self.peer(ahead)} for ahead in range(1, self.count)]


class CubeGather:
    def __init__(self, cube, whole, sems):
        self.cube, self.whole = cube, whole
        self.core_send, self.core_recv, self.far_send, self.far_recv = sems
        self.sibling = cube.sibling()
        self.fars = [cube.far(stage) for stage in range(cube.stages)]

    def to_core(self, block):
        at = self.whole.at[self.cube.owner(block, 0)]
        return remote(at, at, self.core_send.at[block], self.core_recv.at[block], self.sibling)

    def from_core(self, block):
        at = self.whole.at[self.cube.owner(block, 1)]
        return remote(at, at, self.core_send.at[block], self.core_recv.at[block], self.sibling)

    def to_far(self, block, stage):
        slot = block + (1 << stage)
        at = self.whole.at[self.cube.owner(block, 0)]
        return remote(at, at, self.far_send.at[slot], self.far_recv.at[slot], self.fars[stage])

    def from_far(self, slot):
        stage = self.cube.stage_of(slot)
        at = self.whole.at[self.cube.owner(slot, 0)]
        return remote(at, at, self.far_send.at[slot], self.far_recv.at[slot], self.fars[stage])

    def start(self):
        self.to_far(0, 0).start()
        self.to_core(0).start()

    def step(self, block):
        if block:
            self.from_far(block).wait_recv()
            if block == 1:
                for later in range(1, self.cube.stages):
                    self.to_far(0, later).start()
            for later in range(self.cube.stage_of(block) + 1, self.cube.stages):
                self.to_far(block, later).start()
            self.to_core(block).start()

    def step_core(self, block):
        self.from_core(block).wait_recv()

    def close(self):
        for block in range(self.cube.chips):
            self.to_core(block).wait_send()
            if block:
                stage = self.cube.stage_of(block)
                self.to_far(block - (1 << stage), stage).wait_send()


def front_kernel(
    cube, own, gain, cosine, sine, lower, w_query, key_weight, value_weight,
    attn_in_out, weights_out, query_out, pairs_out, mixture_out, log_out, tokens_out,
    slots, attn_in, weights, pairs, sums, heads_low, tokens,
    spread_sems, save, token_send, token_recv, *cube_sems,
):
    count, tok_rows, model_width = slots.shape
    rows, q_width = query_out.shape
    heads = q_width // HEAD_SIZE
    half_size = HEAD_SIZE // 2
    me = cube.index()
    place = lax.axis_index("seq")
    line = Line()
    spread = Spread(line, own, slots, spread_sems)
    weight_gather = CubeGather(cube, weights, cube_sems[:4])
    pair_gather = CubeGather(cube, pairs, cube_sems[4:])
    swap = Swap(heads_low, tokens, token_send, token_recv)
    cuts, first = [], 0
    for weight, share in ((w_query, q_width), (key_weight, HEAD_SIZE), (value_weight, HEAD_SIZE)):
        cuts.append(
            pltpu.make_async_copy(
                weight.at[:, pl.ds(pl.multiple_of(place * share, share), share)],
                weights.at[me, :, pl.ds(first, share)],
                save.at[3 + len(cuts)],
            )
        )
        first += share
    for cut in cuts:
        cut.start()
    greet(cube.partners() + swap.others())

    spread.start()
    for cut in cuts:
        cut.wait()
    weight_gather.start()

    def prepare(slot):
        values = slots[slot].astype(jnp.float32)
        scale = lax.rsqrt(jnp.mean(values * values, axis=-1, keepdims=True) + NORM_EPS)
        attn_in[slot] = (values * scale * (1.0 + gain[...])).astype(jnp.bfloat16)

    def project(slot):
        here = pl.ds(pl.multiple_of(slot * tok_rows, tok_rows), tok_rows)
        cos_part, sin_part = cosine[slot], sine[slot]
        tokens_now = attn_in[slot]

        def turned(first):
            columns = pl.ds(first, HEAD_SIZE)
            values = jnp.dot(
                tokens_now,
                weights[:, :, columns].reshape(model_width, HEAD_SIZE),
                preferred_element_type=jnp.float32,
            )
            left, right = values[:, :half_size], values[:, half_size:]
            return values, jnp.concatenate(
                [left * cos_part - right * sin_part, right * cos_part + left * sin_part], axis=-1
            ).astype(jnp.bfloat16)

        for head in range(heads):
            query_out[here, pl.ds(head * HEAD_SIZE, HEAD_SIZE)] = turned(head * HEAD_SIZE)[1]
        pairs[me, here, :HEAD_SIZE] = turned(q_width)[1]
        pairs[me, here, HEAD_SIZE:] = turned(q_width + HEAD_SIZE)[0].astype(jnp.bfloat16)

    def arrivals(turn, body):
        for way in (1, -1):
            slot = place - way * (turn + 1)

            @pl.when((slot >= 0) & (slot < count))
            def _(slot=slot):
                body(slot)

    prepare(place)
    for block in range(cube.chips // 2):
        weight_gather.step(block)
    spread.forward_turn(1)
    arrivals(0, prepare)
    for block in range(cube.chips // 2, cube.chips):
        weight_gather.step(block)
    for block in range(cube.chips):
        weight_gather.step_core(block)
    save_weights = pltpu.make_async_copy(weights, weights_out, save.at[0])
    save_weights.start()
    project(place)
    arrivals(0, project)
    spread.forward_turn(2)
    arrivals(1, prepare)
    arrivals(1, project)
    spread.forward_turn(3)
    arrivals(2, prepare)
    arrivals(2, project)
    save_attn_in = pltpu.make_async_copy(attn_in, attn_in_out, save.at[1])
    save_attn_in.start()
    pair_gather.start()

    mixture_out[...] = jnp.zeros_like(mixture_out)
    sums[...] = jnp.zeros_like(sums)
    tall = rows // 2

    def attend(owner, head, first):
        columns = pl.ds(pl.multiple_of(head * HEAD_SIZE, HEAD_SIZE), HEAD_SIZE)
        key, value = pairs[owner, :, :HEAD_SIZE], pairs[owner, :, HEAD_SIZE:]
        key_ids = owner * rows + lax.broadcasted_iota(jnp.int32, (1, rows), 1)
        here = pl.ds(first, tall)
        raw = dot_last(query_out[here, columns], key)
        capped = SOFT_CAP * jnp.tanh(raw * (HEAD_SIZE ** (-0.5) / SOFT_CAP))
        row_ids = me * rows + first + lax.broadcasted_iota(jnp.int32, (tall, 1), 0)
        allowed = (key_ids <= row_ids) & (key_ids >= lower[here, :])
        weight = jnp.where(allowed, jnp.exp(capped), 0.0)
        sums[head, here, :] += jnp.sum(weight, axis=-1, keepdims=True)
        mixture_out[here, columns] += jnp.dot(
            weight.astype(jnp.bfloat16), value, preferred_element_type=jnp.float32
        )

    def attend_owner(block, half, firsts):
        owner = cube.owner(block, half)

        @pl.when(owner <= me)
        def _():
            def step(head, carry):
                for first in firsts:
                    attend(owner, head, first)
                return carry

            lax.fori_loop(0, heads, step, 0)

    def finish(first):
        here = pl.ds(first, tall)
        blocks = pl.ds(first // tok_rows, tall // tok_rows)
        for head in range(heads):
            columns = pl.ds(head * HEAD_SIZE, HEAD_SIZE)
            mixed = mixture_out[here, columns] / sums[head, here, :]
            mixture_out[here, columns] = mixed
            heads_low[blocks, :, columns] = mixed.astype(jnp.bfloat16).reshape(
                tall // tok_rows, tok_rows, HEAD_SIZE
            )
            log_out[head, here, :] = jnp.log(sums[head, here, :])
        for ahead in range(1, count):

            @pl.when(swap.peer(ahead) // (tall // tok_rows) == first // tall)
            def _(ahead=ahead):
                swap.start(ahead)

    final = cube.chips - 1
    firsts = range(0, rows, tall)
    for block in range(final):
        pair_gather.step(block)
        attend_owner(block, 0, firsts)
        pair_gather.step_core(block)
        attend_owner(block, 1, firsts)
    pair_gather.step(final)
    for first in firsts:
        attend_owner(final, 0, [first])
        if not first:
            pair_gather.step_core(final)
        attend_owner(final, 1, [first])
        finish(first)
    save_pairs = pltpu.make_async_copy(pairs, pairs_out, save.at[2])
    save_pairs.start()
    swap.keep()
    pair_gather.close()
    weight_gather.close()
    spread.close_sends()
    swap.wait_recv()
    for other in range(count):
        tokens_out[:, pl.ds(other * q_width, q_width)] = tokens[other]
    swap.wait_send()
    save_weights.wait()
    save_attn_in.wait()
    save_pairs.wait()


def front(cube, collective_id, own, projections, gain, cosine, sine, lower):
    count = 4
    tok_rows, width = own.shape
    weight_rows = projections[0].shape[0]
    head_columns = sum(weight.shape[1] for weight in projections) // count
    layer_count = 2 * cube.chips
    rows = count * tok_rows
    q_width = head_columns - 2 * HEAD_SIZE
    heads = q_width // HEAD_SIZE
    low, full = jnp.bfloat16, jnp.float32
    inside = pl.BlockSpec(memory_space=pltpu.VMEM)
    outside = pl.BlockSpec(memory_space=pl.ANY)
    attn_in, weights, query, pairs, mixture, log_total, tokens = pl.pallas_call(
        functools.partial(front_kernel, cube),
        out_shape=[
            jax.ShapeDtypeStruct((count, tok_rows, width), low),
            jax.ShapeDtypeStruct((layer_count, weight_rows, head_columns), low),
            jax.ShapeDtypeStruct((rows, q_width), low),
            jax.ShapeDtypeStruct((layer_count, rows, 2 * HEAD_SIZE), low),
            jax.ShapeDtypeStruct((rows, q_width), full),
            jax.ShapeDtypeStruct((heads, rows, 1), full),
            jax.ShapeDtypeStruct((tok_rows, count * q_width), low),
        ],
        in_specs=[inside] * 5 + [outside] * 3,
        out_specs=[outside, outside, inside, outside, inside, inside, inside],
        scratch_shapes=[
            pltpu.VMEM((count, tok_rows, width), low),
            pltpu.VMEM((count, tok_rows, width), low),
            pltpu.VMEM((layer_count, weight_rows, head_columns), low),
            pltpu.VMEM((layer_count, rows, 2 * HEAD_SIZE), low),
            pltpu.VMEM((heads, rows, 1), full),
            pltpu.VMEM((count, tok_rows, q_width), low),
            pltpu.VMEM((count, tok_rows, q_width), low),
            pltpu.SemaphoreType.DMA((4, 3)),
            pltpu.SemaphoreType.DMA((6,)),
            pltpu.SemaphoreType.DMA((count,)),
            pltpu.SemaphoreType.DMA((count,)),
        ]
        + cube.semaphores(),
        compiler_params=pltpu.CompilerParams(
            collective_id=collective_id,
            has_side_effects=True,
            vmem_limit_bytes=60 * 2**20,
        ),
        cost_estimate=pl.CostEstimate(
            flops=16 * rows * rows * layer_count * q_width,
            bytes_accessed=0,
            transcendentals=0,
        ),
    )(
        own,
        gain.reshape(1, width),
        cosine,
        sine,
        lower.reshape(rows, 1),
        *projections,
    )
    return (
        attn_in.reshape(rows, width),
        weights.reshape(-1, head_columns),
        query,
        pairs.reshape(-1, 2 * HEAD_SIZE),
        mixture,
        log_total.reshape(heads, rows),
        tokens,
    )


def unit_product(left, right, own, unit, skip=0):
    chunk_rows, width = own.shape[1:]
    per_unit = UNIT_ROWS // chunk_rows
    columns = pl.ds(pl.multiple_of((unit + skip) * UNIT_ROWS, UNIT_ROWS), UNIT_ROWS)

    def columns_of(ref, columns):
        values = ref[(slice(None),) * (len(ref.shape) - 1) + (columns,)]
        return values.reshape(-1, values.shape[-1])

    flipped = columns_of(left, columns).T
    for tile in tiles_of(width, 768):
        sums = jnp.dot(flipped, columns_of(right, tile), preferred_element_type=jnp.float32)
        own[pl.ds(unit * per_unit, per_unit), :, tile] = sums.astype(jnp.bfloat16).reshape(
            per_unit, chunk_rows, tile.size
        )


def norm_backward(values, gain, grad):
    scale = lax.rsqrt(jnp.mean(values * values, axis=-1, keepdims=True) + NORM_EPS)
    gained = (1.0 + gain) * grad
    back = scale * gained - values * (
        scale * scale * scale * jnp.mean(values * gained, axis=-1, keepdims=True)
    )
    return back, jnp.sum(values * scale * grad, axis=0, keepdims=True)


def attention_backward_kernel(
    cube, grad_model, mid, branch, cotangent, gain_in, gain_out, mixture, query, log_total, lower,
    tokens, cosine, sine, w_out, pairs_in, left_in, right_in, attn_in, early,
    mid_out, gains_out, grads_out, out_part, column_part, total_out,
    branch_low, wide, left, right, part, from_core, from_far, query_sums, pair_sums, delta, to_heads, heads_in,
    own, from_end, from_middle, line_sems, loads, saves, swap_send, swap_recv,
    back_send, back_recv, sum_send, sum_recv,
):
    rows, width = query.shape
    count, tok_rows, _ = to_heads.shape
    model_width = mid.shape[1]
    heads = width // HEAD_SIZE
    stages, chips = cube.stages, cube.chips
    top = stages - 1
    me = cube.index()
    sibling = cube.sibling()
    fars = [cube.far(stage) for stage in range(stages)]
    line = Line()
    job = LineJob(line, own, from_end, from_middle, from_end, total_out, line_sems)
    job.first = early.shape[0]
    per_unit = UNIT_ROWS // own.shape[1]
    skip = early.shape[0] // per_unit
    swap = Swap(to_heads, heads_in, swap_send, swap_recv)
    row_ids = me * rows + lax.broadcasted_iota(jnp.int32, (1, rows), 1)
    tall = rows // 2
    pair_rows = pairs_in.shape[0]
    load_left = pltpu.make_async_copy(left_in, left, loads.at[0])
    load_right = pltpu.make_async_copy(right_in, right, loads.at[1])
    load_pairs = pltpu.make_async_copy(pairs_in, wide.at[pl.ds(0, pair_rows)], loads.at[2])
    load_out = [
        pltpu.make_async_copy(
            w_out.at[:, pl.ds(block * width, width)],
            wide.at[pl.ds(block * model_width, model_width)],
            loads.at[3 + block],
        )
        for block in range(count)
    ]
    load_attn_in = pltpu.make_async_copy(attn_in, right.at[pl.ds(0, rows)], loads.at[3 + count])

    def saved(target, block, at):
        return pltpu.make_async_copy(
            wide.at[pl.ds(block * model_width, model_width)],
            target.at[:, pl.ds(block * width, width)],
            saves.at[at],
        )

    save_out = [saved(out_part, block, block) for block in range(count)]
    save_columns = [saved(column_part, block, count + block) for block in range(2)]
    move_early = pltpu.make_async_copy(
        early, total_out.at[pl.ds(0, job.first)], loads.at[4 + count]
    )
    load_left.start()
    load_right.start()
    for copy in load_out:
        copy.start()
    move_early.start()

    def sum_to_core(block):
        return remote(
            part.at[block, 1], from_core.at[block], back_send.at[block], back_recv.at[block], sibling
        )

    def sum_to_far(block, stage):
        return remote(
            part.at[block, 0], from_far.at[block], sum_send.at[block], sum_recv.at[block], fars[stage]
        )

    def one_head(owner, head):
        columns = pl.ds(head * HEAD_SIZE, HEAD_SIZE)
        query_head = query[:, columns]
        grad_head = heads_in[:, :, columns].reshape(rows, HEAD_SIZE)
        log_head, delta_head = log_total[head : head + 1, :], delta[head : head + 1, :]
        for first in range(0, rows, tall):
            here = pl.ds(pl.multiple_of(owner * rows, rows) + first, tall)
            key, value = wide[here, :HEAD_SIZE], wide[here, HEAD_SIZE:]
            bent = jnp.tanh(dot_last(key, query_head) * (HEAD_SIZE ** (-0.5) / SOFT_CAP))
            key_ids = owner * rows + first + lax.broadcasted_iota(jnp.int32, (tall, 1), 0)
            allowed = (key_ids <= row_ids) & (key_ids >= lower[...])
            probs = jnp.where(allowed, jnp.exp(SOFT_CAP * bent - log_head), 0.0)
            grad_raw = (
                probs
                * (dot_last(value, grad_head) - delta_head)
                * ((1.0 - bent * bent) * HEAD_SIZE ** (-0.5))
            ).astype(jnp.bfloat16)
            key_sums = jnp.dot(grad_raw, query_head, preferred_element_type=jnp.float32)
            value_sums = jnp.dot(
                probs.astype(jnp.bfloat16), grad_head, preferred_element_type=jnp.float32
            )
            inner = pl.ds(first, tall)
            if head:
                key_sums = key_sums + pair_sums[inner, :HEAD_SIZE]
                value_sums = value_sums + pair_sums[inner, HEAD_SIZE:]
            pair_sums[inner, :HEAD_SIZE] = key_sums
            pair_sums[inner, HEAD_SIZE:] = value_sums
            query_sums[:, columns] += dot_first(grad_raw, key)

    def line_step(at):
        @pl.when(at < job.count)
        def _():
            @pl.when(lax.rem(at, per_unit) == 0)
            def _():
                unit_product(left, right, own, at // per_unit, skip)

            @pl.when(line.is_end)
            def _():
                job.send_end(at)

            @pl.when(jnp.logical_not(line.is_end) & (at >= 1))
            def _():
                job.add_middle(at - 1)

    def turn(step, carry):
        block = chips - 1 - step // 2
        half = 1 - lax.rem(step, 2)
        owner = cube.owner(block, half)

        @pl.when(owner <= me)
        def _():
            for head in range(heads):
                one_head(owner, head)
            part[block, half] = pair_sums[...].astype(jnp.bfloat16)

        @pl.when(owner > me)
        def _():
            part[block, half] = jnp.zeros_like(part[block, half])

        @pl.when(half == 1)
        def _():
            sum_to_core(block).start()

        @pl.when(half == 0)
        def _():
            sum_to_core(block).wait_recv()
            part[block, 0] = (
                part[block, 0].astype(jnp.float32) + from_core[block].astype(jnp.float32)
            ).astype(jnp.bfloat16)

            @pl.when(block >= chips // 2)
            def _():
                sum_to_far(block, top).start()

        line_step(EARLY_STEPS + step)

        @pl.when(step == 2 * chips - 3)
        def _():
            for stage in reversed(range(1, stages)):
                for block in reversed(range(1, 1 << stage)):
                    slot = block + (1 << stage)
                    sum_to_far(slot, stage).wait_recv()
                    part[block, 0] = (
                        part[block, 0].astype(jnp.float32) + from_far[slot].astype(jnp.float32)
                    ).astype(jnp.bfloat16)
                    if cube.stage_of(block) == stage - 1:
                        sum_to_far(block, stage - 1).start()

        return carry

    greet(cube.partners() + swap.others())
    load_left.wait()
    load_right.wait()
    line_step(jnp.int32(0))

    grad_mid, gain_sum = norm_backward(mid[...], gain_in[...], grad_model[...])
    grad_mid = cotangent[...].astype(jnp.float32) + grad_mid
    mid_out[...] = grad_mid
    gains_out[0:1, :] = gain_sum
    grad_branch, gain_sum = norm_backward(branch[...], gain_out[...], grad_mid)
    gains_out[1:2, :] = gain_sum
    branch_low[...] = grad_branch.astype(jnp.bfloat16)
    line_step(jnp.int32(1))
    for copy in load_out:
        copy.wait()
    for ahead in [*range(1, count), 0]:
        peer = swap.peer(ahead)
        here = pl.ds(pl.multiple_of(peer * model_width, model_width), model_width)
        to_heads[peer] = jnp.dot(
            branch_low[...], wide[here, :], preferred_element_type=jnp.float32
        ).astype(jnp.bfloat16)
        if ahead:
            swap.start(ahead)
    load_pairs.start()
    swap.keep()
    query_sums[...] = jnp.zeros_like(query_sums)
    for at in range(2, EARLY_STEPS):
        line_step(jnp.int32(at))
    swap.wait_recv()
    ones = jnp.ones((8, HEAD_SIZE), jnp.float32)
    for head in range(heads):
        columns = pl.ds(head * HEAD_SIZE, HEAD_SIZE)
        product = mixture[:, columns] * heads_in[:, :, columns].reshape(rows, HEAD_SIZE).astype(
            jnp.float32
        )
        delta[head : head + 1, :] = lax.dot_general(
            ones,
            product,
            (((1,), (1,)), ((), ())),
            precision=lax.Precision.HIGHEST,
            preferred_element_type=jnp.float32,
        )[0:1, :]
    load_pairs.wait()
    lax.fori_loop(0, 2 * chips, turn, 0)

    later = range(EARLY_STEPS + 2 * chips, job.count)
    for at in later[:-1]:
        line_step(jnp.int32(at))
    load_attn_in.start()
    for block in range(count):
        columns = pl.ds(block * width, width)
        for tile in tiles_of(model_width, 768):
            here = pl.ds(block * model_width + tile.start, tile.size)
            wide[here, :] = dot_first(branch_low[:, tile], tokens[:, columns]).astype(jnp.bfloat16)
        save_out[block].start()
    for at in later[-1:]:
        line_step(jnp.int32(at))

    total = part[0, 0].astype(jnp.float32)
    for stage in reversed(range(stages)):
        sum_to_far(1 << stage, stage).wait_recv()
        total = total + from_far[1 << stage].astype(jnp.float32)

    @pl.when(jnp.logical_not(line.is_end))
    def _():
        job.add_middle(job.count - 1)

    def turned_back(grads, first):
        grads = grads.astype(jnp.bfloat16).astype(jnp.float32)
        half_size = HEAD_SIZE // 2
        left_half, right_half = grads[:, :half_size], grads[:, half_size:]
        cos_part = cosine[...].reshape(rows, half_size)
        sin_part = sine[...].reshape(rows, half_size)
        grads_out[:, first : first + half_size] = (
            left_half * cos_part + right_half * sin_part
        ).astype(jnp.bfloat16)
        grads_out[:, first + half_size : first + HEAD_SIZE] = (
            right_half * cos_part - left_half * sin_part
        ).astype(jnp.bfloat16)

    for head in range(heads):
        turned_back(query_sums[:, pl.ds(head * HEAD_SIZE, HEAD_SIZE)], head * HEAD_SIZE)
    turned_back(total[:, :HEAD_SIZE], width)
    grads_out[:, width + HEAD_SIZE :] = total[:, HEAD_SIZE:].astype(jnp.bfloat16)
    load_attn_in.wait()
    for block in range(2):
        save_out[block].wait()
        columns = pl.ds(block * width, width)
        for tile in tiles_of(model_width, 768):
            here = pl.ds(block * model_width + tile.start, tile.size)
            wide[here, :] = dot_first(right[:rows, tile], grads_out[:, columns]).astype(jnp.bfloat16)
        save_columns[block].start()

    @pl.when(line.is_end)
    def _():
        job.close_end()

    @pl.when(jnp.logical_not(line.is_end))
    def _():
        job.finish_middle(job.count - 1)
        job.close_middle()

    for copy in save_columns + save_out[2:] + [move_early]:
        copy.wait()
    swap.wait_send()
    for block in range(chips):
        sum_to_core(block).wait_send()
        if block:
            sum_to_far(block, cube.stage_of(block)).wait_send()


def attention_backward(
    cube, collective_id, grad_model, mid, branch, cotangent, gain_in, gain_out, mixture, query,
    log_total, lower, tokens, cosine, sine, w_out, pairs, left, right, attn_in, early,
):
    count = 4
    tok_rows, model_width = mid.shape
    rows, width = query.shape
    pair_width = pairs.shape[1]
    chips = cube.chips
    heads = width // HEAD_SIZE
    units, ffn_width = left.shape[1], right.shape[1]
    low, full = jnp.bfloat16, jnp.float32
    all_chunks = (units // CHUNK_ROWS, CHUNK_ROWS, ffn_width)
    chunks = (all_chunks[0] - early.shape[0],) + all_chunks[1:]
    inside = pl.BlockSpec(memory_space=pltpu.VMEM)
    outside = pl.BlockSpec(memory_space=pl.ANY)
    wide_rows = max(count * model_width, pairs.shape[0])
    grad_mid, gains, head_grads, out_part, column_part, total = pl.pallas_call(
        functools.partial(attention_backward_kernel, cube),
        out_shape=[
            jax.ShapeDtypeStruct((tok_rows, model_width), full),
            jax.ShapeDtypeStruct((2, model_width), full),
            jax.ShapeDtypeStruct((rows, width + pair_width), low),
            jax.ShapeDtypeStruct((model_width, count * width), low),
            jax.ShapeDtypeStruct((model_width, width + pair_width), low),
            jax.ShapeDtypeStruct(all_chunks, low),
        ],
        in_specs=[inside] * 13 + [outside] * 6,
        out_specs=[inside] * 3 + [outside] * 3,
        scratch_shapes=[
            pltpu.VMEM((tok_rows, model_width), low),
            pltpu.VMEM((wide_rows, width), low),
            pltpu.VMEM(left.shape, low),
            pltpu.VMEM(right.shape, low),
            pltpu.VMEM((chips, 2, rows, pair_width), low),
            pltpu.VMEM((chips, rows, pair_width), low),
            pltpu.VMEM((chips, rows, pair_width), low),
            pltpu.VMEM((rows, width), full),
            pltpu.VMEM((rows, pair_width), full),
            pltpu.VMEM((heads, rows), full),
            pltpu.VMEM((count, tok_rows, width), low),
            pltpu.VMEM((count, tok_rows, width), low),
            pltpu.VMEM(chunks, low),
            pltpu.VMEM(chunks, low),
            pltpu.VMEM(chunks, low),
            pltpu.SemaphoreType.DMA((7, chunks[0])),
            pltpu.SemaphoreType.DMA((5 + count,)),
            pltpu.SemaphoreType.DMA((2 + count,)),
            pltpu.SemaphoreType.DMA((count,)),
            pltpu.SemaphoreType.DMA((count,)),
        ]
        + [pltpu.SemaphoreType.DMA((chips,))] * 4,
        compiler_params=pltpu.CompilerParams(
            collective_id=collective_id,
            has_side_effects=True,
            vmem_limit_bytes=63 * 2**20,
        ),
        cost_estimate=pl.CostEstimate(
            flops=64 * left.shape[0] * units * ffn_width, bytes_accessed=0, transcendentals=0
        ),
    )(
        grad_model,
        mid,
        branch,
        cotangent,
        gain_in.reshape(1, -1),
        gain_out.reshape(1, -1),
        mixture,
        query,
        log_total,
        lower.reshape(1, rows),
        tokens,
        cosine,
        sine,
        w_out,
        pairs,
        left,
        right,
        attn_in,
        early,
    )
    return grad_mid, gains, head_grads, out_part, column_part, total.reshape(units, ffn_width)


class TokenGrads:
    def __init__(self, ins, outs, scratch):
        self.swapped, *self.projections, self.inputs, self.grad_mid, self.gain = ins
        self.grad_inputs, self.gain_sum = outs
        *self.whole, self.landed, self.sums, self.rows, loads, send_sems, recv_sems = scratch
        self.swap = Swap(self.swapped, self.landed, send_sems, recv_sems)
        self.loads = [
            pltpu.make_async_copy(source, target, loads.at[at])
            for at, (source, target) in enumerate(zip(self.projections, self.whole))
        ]
        self.tile = 768
        self.steps = self.sums.shape[1] // self.tile

    def start(self):
        for ahead in range(1, self.swap.count):
            self.swap.start(ahead)
        self.swap.keep()
        for copy in self.loads:
            copy.start()

    def step(self, at):
        @pl.when(at == 0)
        def _():
            self.swap.wait_recv()
            for copy in self.loads:
                copy.wait()
            count = self.swap.count
            first, start = 0, 0
            for weight in self.whole:
                share = weight.shape[1] // count
                for block in range(count):
                    self.rows[:, pl.ds(start + block * share, share)] = self.landed[
                        block, :, pl.ds(first, share)
                    ]
                first, start = first + share, start + count * share

        @pl.when(at >= 0)
        def _():
            features = pl.ds(pl.multiple_of(at * self.tile, self.tile), self.tile)
            start, total = 0, 0.0
            for weight in self.whole:
                total = total + dot_last(
                    self.rows[:, pl.ds(start, weight.shape[1])], weight[features, :]
                )
                start += weight.shape[1]
            self.sums[:, features] = total

    def close(self):
        back, self.gain_sum[...] = norm_backward(
            self.inputs[...].astype(jnp.float32), self.gain[...], self.sums[...]
        )
        self.grad_inputs[...] = self.grad_mid[...] + back
        self.swap.wait_send()


def summed_products_kernel(cube, shares, given_count, spread_count, token_count, *refs):
    refs = list(refs)
    left, right = refs[:2]
    given = refs[2 : 2 + given_count]
    blocks = refs[2 + given_count : 2 + given_count + spread_count]
    refs = refs[2 + given_count + spread_count :]
    token_ins, refs = refs[: 7 * token_count], refs[7 * token_count :]
    if cube:
        small, refs = refs[0], refs[1:]
    outs = refs[: 1 + given_count]
    spread_outs = refs[1 + given_count : 1 + given_count + spread_count]
    refs = refs[1 + given_count + spread_count :]
    token_outs, scratch = refs[: 2 * token_count], refs[2 * token_count :]
    if cube:
        small_out, scratch = scratch[0], scratch[1:]
    line = Line()
    jobs = [
        LineJob(line, *scratch[4 * at : 4 * at + 3], scratch[4 * at + 1], outs[at], scratch[4 * at + 3])
        for at in range(given_count + 1)
    ]
    scratch = scratch[4 * (given_count + 1) :]
    spreads = [
        Spread(
            line, blocks[at], *scratch[3 * at : 3 * at + 2], spread_outs[at], shares,
            scratch[3 * at + 2],
        )
        for at in range(spread_count)
    ]
    scratch = scratch[3 * spread_count :]
    token_scratch, scratch = scratch[: 9 * token_count], scratch[9 * token_count :]
    token = TokenGrads(token_ins, token_outs, token_scratch) if token_count else None
    if cube:
        small_sum, small_in, small_slots, small_send, small_recv, small_spread_sems = scratch
        small_spread = Spread(line, small_sum, small_slots, small_spread_sems)
        cube_devices = [cube.device_across(bit) for bit in [cube.ctx_count] + cube.far_bits]
    for job, before in zip(jobs[1:], jobs):
        job.before = before
    product = jobs[-1]
    per_unit = UNIT_ROWS // product.own.shape[1]

    def each_unit(body):
        def step(unit, carry):
            unit_product(left, right, product.own, unit)
            for part in range(per_unit):
                body(unit * per_unit + part)
            if token:
                token.step(unit - (product.count // per_unit - token.steps))
            return carry

        lax.fori_loop(0, product.count // per_unit, step, 0)

    greet(
        [{"seq": lax.rem(line.place + ahead, 4)} for ahead in range(1, 4)]
        + (cube_devices if cube else [])
    )
    if token:
        token.start()
    for spread in spreads:
        spread.start()
    for array, job in zip(given, jobs):
        job.own[...] = array[...]
    if cube:
        small_sum[...] = small[...]
        for at, device in enumerate(cube_devices):
            copy = remote(
                small_sum, small_in.at[at], small_send.at[at], small_recv.at[at], device
            )
            copy.start()
            copy.wait()
            small_sum[...] += small_in[at]
        small_spread.start()
        spreads = spreads + [small_spread]

    @pl.when(line.is_end)
    def _():
        for job in jobs[:-1]:
            job.each(job.send_end)
        each_unit(product.send_end)
        for spread in spreads:
            spread.forward()
        for job in jobs:
            job.close_end()

    @pl.when(jnp.logical_not(line.is_end))
    def _():
        for spread in spreads:
            spread.forward_turn(1)
        for job in jobs[:-1]:
            job.each(job.add_middle)
        for spread in spreads:
            spread.forward_turn(2)
        each_unit(product.add_middle)
        product.finish_middle(product.count - 1)
        for job in jobs:
            job.close_middle()

    for spread in spreads:
        spread.close()
    if cube:
        small_out[...] = sum(small_slots[at] for at in range(4))
    if token:
        token.close()


def summed_products(
    collective_id, left, right, given=(), blocks=(), shares=(), token=(), small=None, cube=None
):
    rows, units = left.shape
    width = right.shape[1]
    low = jnp.bfloat16
    shapes = [
        (array.shape[0] // GIVEN_ROWS, GIVEN_ROWS, array.shape[1]) for array in given
    ] + [(units // SHORT_CHUNK_ROWS, SHORT_CHUNK_ROWS, width)]
    spreads = [(4,) + block.shape for block in blocks]
    scratch = []
    for shape in shapes:
        scratch += [pltpu.VMEM(shape, low)] * 3 + [pltpu.SemaphoreType.DMA((7, shape[0]))]
    for shape in spreads:
        scratch += [
            pltpu.VMEM(shape, low),
            pltpu.SemaphoreType.DMA((4, 3)),
            pltpu.SemaphoreType.DMA((4 * len(shares),)),
        ]
    spread_outs = [(block.shape[0], 4 * block.shape[1]) for block in blocks]
    out_shapes = [jax.ShapeDtypeStruct(shape, low) for shape in shapes + spread_outs]
    token_specs = []
    inside = pl.BlockSpec(memory_space=pltpu.VMEM)
    outside = pl.BlockSpec(memory_space=pl.ANY)
    outer_count = len(out_shapes)
    if token:
        swapped, projections, inputs = token[0], token[1:4], token[4]
        tok_rows, model_width = inputs.shape
        out_shapes += [
            jax.ShapeDtypeStruct((tok_rows, model_width), jnp.float32),
            jax.ShapeDtypeStruct((1, model_width), jnp.float32),
        ]
        token_specs = [inside] + [outside] * 3 + [inside] * 3
        scratch += [pltpu.VMEM(projection.shape, low) for projection in projections]
        scratch += [
            pltpu.VMEM(swapped.shape, low),
            pltpu.VMEM((tok_rows, model_width), jnp.float32),
            pltpu.VMEM((tok_rows, swapped.shape[0] * swapped.shape[2]), low),
            pltpu.SemaphoreType.DMA((3,)),
            pltpu.SemaphoreType.DMA((4,)),
            pltpu.SemaphoreType.DMA((4,)),
        ]
    extra = []
    if cube:
        extra = [small]
        out_shapes.append(jax.ShapeDtypeStruct(small.shape, small.dtype))
        partners = 1 + cube.stages
        scratch += [
            pltpu.VMEM(small.shape, small.dtype),
            pltpu.VMEM((partners,) + small.shape, small.dtype),
            pltpu.VMEM((4,) + small.shape, small.dtype),
            pltpu.SemaphoreType.DMA((partners,)),
            pltpu.SemaphoreType.DMA((partners,)),
            pltpu.SemaphoreType.DMA((4, 3)),
        ]
    totals = pl.pallas_call(
        functools.partial(
            summed_products_kernel, cube, shares, len(given), len(blocks), 1 if token else 0
        ),
        out_shape=out_shapes,
        in_specs=[inside] * (2 + len(given) + len(blocks))
        + token_specs
        + [inside] * len(extra),
        out_specs=[outside] * outer_count + [inside] * (len(out_shapes) - outer_count),
        scratch_shapes=scratch,
        compiler_params=pltpu.CompilerParams(
            collective_id=collective_id,
            has_side_effects=True,
            vmem_limit_bytes=60 * 2**20,
        ),
        cost_estimate=pl.CostEstimate(
            flops=64 * rows * units * width, bytes_accessed=0, transcendentals=0
        ),
    )(left, right, *(array.reshape(shape) for array, shape in zip(given, shapes)), *blocks, *token, *extra)
    count = len(shapes)
    return [total.reshape(-1, total.shape[-1]) for total in totals[:count]] + list(totals[count:])


def per_device(
    inputs,
    positions,
    w_query,
    key_weight,
    value_weight,
    w_out,
    w_gate,
    w_up,
    w_down,
    gain_attn_in,
    gain_attn_out,
    gain_ffn_in,
    gain_ffn_out,
    cotangent,
):
    layer = ("dp", "ctx")
    tok_rows, model_width = inputs.shape
    seq_count = lax.axis_size("seq")
    seq_index = lax.axis_index("seq")
    cycle_count = lax.axis_size(layer)
    cycle_index = lax.axis_index(layer)
    block_rows = tok_rows * seq_count
    q_width = w_query.shape[1]
    kv_width = key_weight.shape[1]
    q_cols = q_width // seq_count
    kv_cols = kv_width // seq_count
    local_q = q_cols // HEAD_SIZE
    local_kv = kv_cols // HEAD_SIZE
    grouping_factor = local_q // local_kv
    back_blocks = min((WINDOW - 2 + block_rows) // block_rows, cycle_count - 1)
    score_scale = HEAD_SIZE ** (-0.5)

    full_out = gathered(w_out, layer)
    full_key = gathered(key_weight, layer)
    cos_part, sin_part = angles(positions, HEAD_SIZE)
    residual = inputs.astype(jnp.float32)
    row_ids = cycle_index * block_rows + jnp.arange(block_rows, dtype=jnp.int32)
    lower_ids = row_ids - jnp.minimum(positions, WINDOW - 1)
    dp_count, ctx_count = lax.axis_size("dp"), lax.axis_size("ctx")
    fused = (
        seq_count == 4
        and local_kv == 1
        and cube_fits(dp_count, ctx_count, tok_rows, w_gate.shape[0], model_width)
    )
    if fused:
        cube = Cube(dp_count, ctx_count)
        turns = [part.reshape(seq_count, tok_rows, -1) for part in (cos_part, sin_part)]
        block_attn_in, head_weights, query_heads, all_pairs, attn_f32, log_total, out_tok = front(
            cube, 6, inputs, (w_query, key_weight, value_weight), gain_attn_in, *turns, lower_ids
        )
    else:
        own_columns = jnp.concatenate(
            [
                lax.dynamic_slice_in_dim(w_query, seq_index * q_cols, q_cols, 1),
                lax.dynamic_slice_in_dim(key_weight, seq_index * kv_cols, kv_cols, 1),
                lax.dynamic_slice_in_dim(value_weight, seq_index * kv_cols, kv_cols, 1),
            ],
            axis=1,
        )
        block_inputs = gathered(inputs, "seq")
        head_weights = gathered(own_columns, layer)

        block_attn_in = normed(block_inputs.astype(jnp.float32), gain_attn_in).astype(jnp.bfloat16)
        projected = jnp.dot(block_attn_in, head_weights, preferred_element_type=jnp.float32)
        query_heads = rotate(
            projected[:, :q_cols].reshape(block_rows, local_q, HEAD_SIZE), cos_part, sin_part
        ).astype(jnp.bfloat16)
        key_heads = rotate(
            projected[:, q_cols : q_cols + kv_cols].reshape(block_rows, local_kv, HEAD_SIZE),
            cos_part,
            sin_part,
        ).astype(jnp.bfloat16)
        value_heads = projected[:, q_cols + kv_cols :].astype(jnp.bfloat16)
        own_pair = jnp.concatenate([key_heads.reshape(block_rows, kv_cols), value_heads], axis=1)
        all_pairs = gathered(own_pair, layer)
        query_grouped = query_heads.reshape(block_rows, local_kv, grouping_factor, HEAD_SIZE)

        def pair_at(offset):
            if offset == 0:
                pair = own_pair
            else:
                pair = lax.dynamic_slice_in_dim(
                    all_pairs, jnp.maximum(cycle_index - offset, 0) * block_rows, block_rows, 0
                )
            return (
                pair[:, :kv_cols].reshape(block_rows, local_kv, HEAD_SIZE),
                pair[:, kv_cols:].reshape(block_rows, local_kv, HEAD_SIZE),
            )

        kv_pairs = [pair_at(offset) for offset in range(back_blocks + 1)]

        def block_scores(key_rows, offset):
            raw_scores = jnp.einsum(
                "rkgd,ckd->kgrc", query_grouped, key_rows, preferred_element_type=jnp.float32
            )
            capped = SOFT_CAP * jnp.tanh(raw_scores * score_scale / SOFT_CAP)
            col_ids = (cycle_index - offset) * block_rows + jnp.arange(block_rows, dtype=jnp.int32)
            allowed = (col_ids[None, :] <= row_ids[:, None]) & (col_ids[None, :] >= lower_ids[:, None])
            return (capped, allowed)

        capped, allowed = block_scores(kv_pairs[0][0], 0)
        row_top = jnp.max(jnp.where(allowed, capped, -1e30), axis=-1)
        running_sum = jnp.sum(jnp.where(allowed, jnp.exp(capped - row_top[..., None]), 0.0), axis=-1)
        for offset in range(1, back_blocks + 1):
            capped, allowed = block_scores(kv_pairs[offset][0], offset)
            new_top = jnp.maximum(row_top, jnp.max(jnp.where(allowed, capped, -1e30), axis=-1))
            running_sum = running_sum * jnp.exp(row_top - new_top) + jnp.sum(
                jnp.where(allowed, jnp.exp(capped - new_top[..., None]), 0.0), axis=-1
            )
            row_top = new_top
        log_total = row_top + jnp.log(running_sum)
        mixture = jnp.zeros((block_rows, local_kv, grouping_factor, HEAD_SIZE), jnp.float32)
        for offset in range(back_blocks + 1):
            capped, allowed = block_scores(kv_pairs[offset][0], offset)
            probs_low = jnp.where(allowed, jnp.exp(capped - log_total[..., None]), 0.0).astype(
                jnp.bfloat16
            )
            mixture = mixture + jnp.einsum(
                "kgrc,ckd->rkgd", probs_low, kv_pairs[offset][1], preferred_element_type=jnp.float32
            )
        attn_f32 = mixture.reshape(block_rows, q_cols)
        out_tok = lax.all_to_all(
            attn_f32.astype(jnp.bfloat16), "seq", split_axis=0, concat_axis=1, tiled=True
        )
    branch = dot_last(out_tok, full_out)
    mid = residual + normed(branch, gain_attn_out)

    weights = (w_gate, w_up, w_down)
    ffn_own = normed(mid, gain_ffn_in).astype(jnp.bfloat16)
    (ffn_own,) = after((ffn_own,), (full_key,))
    if fused:
        ffn_out, ffn_in, hidden, activated, slope = ffn_call(
            ffn_forward_kernel, cube, 1, ffn_own, weights, (), 3
        )
    else:
        ffn_in = gathered(ffn_own, layer)
        gate_pre = dot_last(ffn_in, w_gate)
        up_pre = dot_last(ffn_in, w_up)
        activated, gelu_pull = jax.vjp(gelu_tanh, gate_pre)
        slope = gelu_pull(up_pre)[0]
        hidden = (activated * up_pre).astype(jnp.bfloat16)
        ffn_out = scattered(jnp.dot(hidden, w_down, preferred_element_type=jnp.float32), layer)
    grad_out = cotangent.astype(jnp.float32)
    ffn_norm, pull_ffn = jax.vjp(normed, ffn_out, gain_ffn_out)
    output = mid + ffn_norm
    grad_ffn, grad_gain_ffn_out = pull_ffn(grad_out)
    grad_ffn_own = grad_ffn.astype(jnp.bfloat16)
    if fused:
        grad_model, grad_ffn_low, grad_gate, grad_up, early_down = ffn_call(
            ffn_backward_kernel, cube, 2, grad_ffn_own, weights, (activated, slope), 2, (hidden,)
        )
        early_down = early_down.reshape(-1, CHUNK_ROWS, model_width)
    else:
        grad_ffn_low = gathered(grad_ffn_own, layer)
        grad_hidden = dot_last(grad_ffn_low, w_down)
        grad_gate = (grad_hidden * slope).astype(jnp.bfloat16)
        grad_up = (grad_hidden * activated).astype(jnp.bfloat16)
        grad_model = scattered(
            jnp.dot(grad_gate, w_gate, preferred_element_type=jnp.float32)
            + jnp.dot(grad_up, w_up, preferred_element_type=jnp.float32),
            layer,
        )
    ffn_in, grad_ffn_low, hidden, grad_gate, grad_up = (
        rows.reshape(-1, rows.shape[-1])
        for rows in (ffn_in, grad_ffn_low, hidden, grad_gate, grad_up)
    )
    if fused:
        grad_mid, gains, head_grads, grad_w_out_part, column_part, grad_w_down = attention_backward(
            cube, 3, grad_model, mid, branch, cotangent, gain_ffn_in, gain_attn_out, attn_f32,
            query_heads, log_total, lower_ids, out_tok, *turns, full_out, all_pairs, hidden, grad_ffn_low,
            block_attn_in, early_down,
        )
        grad_gain_ffn_in, grad_gain_attn_out = gains[0], gains[1]
    else:
        mid_norm, pull_mid = jax.vjp(normed, mid, gain_ffn_in)
        grad_mid_part, grad_gain_ffn_in = pull_mid(grad_model)
        grad_mid = grad_out + grad_mid_part
        branch_norm, pull_branch = jax.vjp(normed, branch, gain_attn_out)
        grad_branch, grad_gain_attn_out = pull_branch(grad_mid)
        grad_branch_low = grad_branch.astype(jnp.bfloat16)
        grad_attn_tok = jnp.dot(grad_branch_low, full_out, preferred_element_type=jnp.float32).astype(
            jnp.bfloat16
        )
        grad_attn_heads = lax.all_to_all(grad_attn_tok, "seq", split_axis=1, concat_axis=0, tiled=True)
        grad_grouped = grad_attn_heads.reshape(block_rows, local_kv, grouping_factor, HEAD_SIZE)
        out_grouped = attn_f32.reshape(block_rows, local_kv, grouping_factor, HEAD_SIZE)
        row_delta = jnp.transpose(
            jnp.sum(grad_grouped.astype(jnp.float32) * out_grouped, axis=-1), (1, 2, 0)
        )
        grad_query = jnp.zeros((block_rows, local_kv, grouping_factor, HEAD_SIZE), jnp.float32)
        kv_grads = jnp.zeros(((back_blocks + cycle_count) * block_rows, 2 * kv_cols), jnp.bfloat16)
        for offset in range(back_blocks, -1, -1):
            key_rows, value_rows = kv_pairs[offset]
            capped, allowed = block_scores(key_rows, offset)
            probs = jnp.where(allowed, jnp.exp(capped - log_total[..., None]), 0.0)
            grad_value = jnp.einsum(
                "kgrc,rkgd->ckd",
                probs.astype(jnp.bfloat16),
                grad_grouped,
                preferred_element_type=jnp.float32,
            )
            grad_probs = jnp.einsum(
                "rkgd,ckd->kgrc", grad_grouped, value_rows, preferred_element_type=jnp.float32
            )
            cap_ratio = capped / SOFT_CAP
            grad_raw = (
                probs
                * (grad_probs - row_delta[..., None])
                * (1.0 - cap_ratio * cap_ratio)
                * score_scale
            ).astype(jnp.bfloat16)
            grad_query = grad_query + jnp.einsum(
                "kgrc,ckd->rkgd", grad_raw, key_rows, preferred_element_type=jnp.float32
            )
            grad_key = jnp.einsum(
                "kgrc,rkgd->ckd", grad_raw, query_grouped, preferred_element_type=jnp.float32
            )
            grad_term = jnp.concatenate(
                [grad_key.reshape(block_rows, kv_cols), grad_value.reshape(block_rows, kv_cols)], axis=1
            )
            kv_grads = lax.dynamic_update_slice_in_dim(
                kv_grads,
                grad_term.astype(jnp.bfloat16),
                (cycle_index - offset + back_blocks) * block_rows,
                0,
            )
        kv_share = scattered_low(kv_grads[back_blocks * block_rows :], layer)
        grad_query = grad_query.reshape(block_rows, q_cols).astype(jnp.bfloat16)
        grad_w_down = summed(dot_first(hidden, grad_ffn_low), "seq")
        grad_w_out_part = dot_first(grad_branch_low, out_tok).astype(jnp.bfloat16)
        kv_share = kv_share.astype(jnp.float32)
        grad_q_pre = rotate_back(
            grad_query.astype(jnp.float32).reshape(block_rows, local_q, HEAD_SIZE),
            cos_part,
            sin_part,
        ).reshape(block_rows, q_cols)
        grad_k_pre = rotate_back(
            kv_share[:, :kv_cols].reshape(block_rows, local_kv, HEAD_SIZE), cos_part, sin_part
        ).reshape(block_rows, kv_cols)
        head_grads = jnp.concatenate([grad_q_pre, grad_k_pre, kv_share[:, kv_cols:]], axis=1).astype(
            jnp.bfloat16
        )
        column_part = dot_first(block_attn_in, head_grads).astype(jnp.bfloat16)
    if fused:
        full_query, full_value = (
            gathered(weight, layer) for weight in after((w_query, value_weight), (grad_model,))
        )
        full_weights = [full_query, full_key, full_value]
        grad_w_gate, grad_inputs, grad_gain_attn_in = summed_products(
            4,
            *after(
                (grad_gate, ffn_in),
                (grad_w_down, column_part, grad_w_out_part, *full_weights),
            ),
            token=(
                head_grads.reshape(seq_count, tok_rows, -1),
                *full_weights,
                inputs,
                grad_mid,
                gain_attn_in.reshape(1, -1),
            ),
        )
        grad_gain_attn_in = grad_gain_attn_in[0]
    else:
        grad_w_gate = summed(dot_first(grad_gate, ffn_in), "seq")
        grad_attn_in = scattered(dot_last(head_grads, head_weights), "seq")
        in_norm, pull_in = jax.vjp(normed, residual, gain_attn_in)
        grad_res_part, grad_gain_attn_in = pull_in(grad_attn_in)
        grad_inputs = grad_mid + grad_res_part
    grad_w_out, column_share = after(
        (scattered_low(grad_w_out_part, layer), scattered_low(column_part, layer)), (grad_w_gate,)
    )
    gain_rows = jnp.stack(
        [grad_gain_attn_in, grad_gain_attn_out, grad_gain_ffn_in, grad_gain_ffn_out]
    )
    if fused:
        grad_w_out, grad_w_up, column_grads, gain_grads = summed_products(
            5,
            *after((grad_up, ffn_in), (grad_w_gate, grad_inputs)),
            (grad_w_out,),
            (column_share,),
            (q_cols, kv_cols, kv_cols),
            small=gain_rows,
            cube=cube,
        )
    else:
        grad_w_up = summed(dot_first(grad_up, ffn_in), "seq")
        grad_w_out = summed(grad_w_out, "seq")
        column_grads = jnp.concatenate(
            [
                lax.all_gather(column_share[:, first : first + share], "seq", axis=1, tiled=True)
                for first, share in ((0, q_cols), (q_cols, kv_cols), (q_cols + kv_cols, kv_cols))
            ],
            axis=1,
        )
        gain_grads = lax.psum(gain_rows, ("dp", "ctx", "seq"))
    column_grads = column_grads.astype(jnp.float32)
    grad_w_gate, grad_w_down = after((grad_w_gate, grad_w_down), (grad_w_up,))
    grad_w_out, grad_w_gate, grad_w_up, grad_w_down = (
        grad.astype(jnp.float32) for grad in (grad_w_out, grad_w_gate, grad_w_up, grad_w_down)
    )
    return (
        output,
        grad_inputs,
        column_grads[:, :q_width],
        column_grads[:, q_width : q_width + kv_width],
        column_grads[:, q_width + kv_width :],
        grad_w_out,
        grad_w_gate,
        grad_w_up,
        grad_w_down,
        gain_grads[0],
        gain_grads[1],
        gain_grads[2],
        gain_grads[3],
    )


def solution(mesh):
    placed = (
        P(("dp", "ctx", "seq"), None),
        P(("dp", "ctx")),
        P(("dp", "ctx"), None),
        P(("dp", "ctx"), None),
        P(("dp", "ctx"), None),
        P(("dp", "ctx"), None),
        P(("dp", "ctx"), None),
        P(("dp", "ctx"), None),
        P(("dp", "ctx"), None),
        P(),
        P(),
        P(),
        P(),
        P(("dp", "ctx", "seq"), None),
    )
    return jax.shard_map(
        per_device,
        mesh=mesh,
        in_specs=placed,
        out_specs=(
            P(("dp", "ctx", "seq"), None),
            P(("dp", "ctx", "seq"), None),
            P(("dp", "ctx"), None),
            P(("dp", "ctx"), None),
            P(("dp", "ctx"), None),
            P(("dp", "ctx"), None),
            P(("dp", "ctx"), None),
            P(("dp", "ctx"), None),
            P(("dp", "ctx"), None),
            P(),
            P(),
            P(),
            P(),
        ),
        check_vma=False,
    )
```

time: 2790 us -> 850 us (0.30)
  waiting for transfers between devices: 2200 us -> 1.55 us
  Pallas kernels: 0 us -> 777 us
  matrix products: 347 us -> 7.41 us
  starting transfers between devices: 75.5 us -> 0.24 us
  blocking collectives: 59.6 us -> 0 us
    reduce_scatter x5 -> x2, waiting for transfers between devices: 806 us -> 0.04 us  [scattered_low(): lax.psum_scatter(array.astype(jnp.bfloat16), axes, scatter_dimension=0, t...]
    pallas_call x0 -> x6, Pallas kernels: none -> 777 us  [the longest x2 361 us: summed_products(): pl.pallas_call(functools.partial(summed_products_kernel, cube, shares, le...]
    psum x1 -> x0, waiting for transfers between devices: 593 us -> none  [per_device(): lax.psum(shares[0].astype(jnp.bfloat16), 'seq').astype(jnp.float32)]
    all_gather x7 -> x4, waiting for transfers between devices: 537 us -> 0.06 us  [gathered(): return lax.all_gather(array, axes, axis=0, tiled=True)]
    dot_general x60 -> x0, matrix products: 245 us -> none  [the longest x5 82.8 us: dot_first(): lax.dot_general(left_rows, right_rows, (((0,), (0,)), ((), ())), preferre...]
    ppermute x14 -> x0, waiting for transfers between devices: 217 us -> none  [passed_along(): return lax.ppermute(array, axis, pairs)]
    dot_general x7 -> x1, matrix products: 102 us -> 7.41 us  [dot_last(): lax.dot_general(left_rows, right_rows, (((1,), (1,)), ((), ())), preferre...]
    psum x1 -> x0, blocking collectives: 44.5 us -> none  [per_device(): lax.psum((grad_gain_attn_in, grad_gain_attn_out, grad_gain_ffn_in, grad_g...]
  transfers between devices with their start and end apart: 34 -> 6, of which waited for: 28 -> 0; matrix products, arithmetic and copies ran while one was open for 11% -> 2% of each run, Pallas kernels for 0% -> 48%
where the time goes in v1:
time: 850 us; the launch traced here: 842 us
  Pallas kernels  777 us (91%)
  other arithmetic  28.4 us (3%)
  between operations  14.7 us (2%)
  local copies, waits for them, and re-layouts  12.7 us (1%)
    pallas_call x2, Pallas kernels, summed_products(): pl.pallas_call(functools.partial(summed_products_kernel, cube, shares, le...  361 us
    pallas_call x2, Pallas kernels, ffn_call(): pl.pallas_call(functools.partial(kernel, cube), out_shape=[jax.ShapeDtype...  172 us
    pallas_call x1, Pallas kernels, attention_backward(): pl.pallas_call(functools.partial(attention_backward_kernel, cube), out_sh...  133 us
    pallas_call x1, Pallas kernels, front(): pl.pallas_call(functools.partial(front_kernel, cube), out_shape=[jax.Shap...  111 us
    convert_element_type x4, other arithmetic, per_device(): grad.astype(jnp.float32)  17.1 us
  transfers between devices with their start and end apart: 6, of which 0 were waited for; matrix products, arithmetic and copies ran while one was open for 2% of the time, Pallas kernels for 48%

profile of v1, /device:TPU:0, one launch (start us, length us, event | category | flops | bytes accessed | tf_op | source)
XLA Modules:
  0.0 841.8 jit_solution(16180091779640520846)
XLA Ops:
  7.2 0.0 copy-start.19
  7.2 0.0 copy-start.18
  7.2 0.0 copy-start.17
  7.2 0.0 all-gather.5.cloned.1.call-start
  7.3 0.7 all-gather.5.cloned.1.call-update
  8.0 0.0 all-gather.7.cloned.1.call-start
  8.0 0.7 all-gather.7.cloned.1.call-update
  8.7 0.0 all-gather.11.cloned.1.call-start
  8.8 0.1 mul.127
  8.9 0.6 reshape.152.gain.refs_8_
  9.5 0.9 reshape.173.lower
  10.4 2.1 multiply_sine_fusion
  12.5 111.2 %shard_map.237 = (bf16[4,160,2304]{2,1,0:T(8,128)(2,1)}, bf16[8,288,1024]{2,1,0:T(8,128)(2,1)}, bf16[640,512]{1,0:T(8,128)(2,1)}, bf16[8,640,512]{2,1,0:T(8,128)...) custom-call(bf16[160,2304]{1,0:T(8,128)(2,1)} %refs_6_.1, ...), custom_call_target="tpu_custom_call" | custom-call | flops 26843545600 | tf_op jit(solution)/shard_map/pallas_call | solution.py:965
  123.7 0.0 all-gather.5.cloned.1.call-done.w_out
  123.7 0.0 copy-start.7
  123.7 7.4 multiply_reduce_fusion.2
  131.1 0.0 copy-start.3
  131.2 0.4 multiply_reduce_fusion.1
  131.6 0.6 copy-done.3
  132.3 1.3 multiply_convert_fusion.own
  133.6 76.7 %shard_map.238 = (f32[160,2304]{1,0:T(8,128)}, bf16[4,2,160,2304]{3,2,1,0:T(8,128)(2,1)}, bf16[4,320,1152]{2,1,0:T(8,128)(2,1)}, bf16[4,320,1152]{2,1,0:T(8,128)(2,1)}, bf16[4,320,1152]{2,1,0:T(8,128)(2,1)}) custom-call(bf16[160,2304]{1,0:T(8,128)(2,1)} %multiply_convert_fusion.own, bf16[1152,2304]{1,0:T(8,128)(2,1)} %w_gate.3, bf16[1152,2304]{1,0:T(8,128)(2,1)} %w_up.3, ...), custom_call_target="tpu_custom_call" | custom-call | flops 20384317440 | bytes 24772608 | tf_op jit(solution)/shard_map/pallas_call | solution.py:482
  210.2 1.7 multiply_reduce_fusion
  211.9 0.1 copy-done
  212.1 1.3 fusion.3
  213.3 2.3 fusion.4
  215.6 95.1 %shard_map.239 = (f32[160,2304]{1,0:T(8,128)}, bf16[4,2,160,2304]{3,2,1,0:T(8,128)(2,1)}, bf16[4,320,1152]{2,1,0:T(8,128)(2,1)}, bf16[4,320,1152]{2,1,0:T(8,128)(2,1)}, bf16[8,32,2304]{2,1,0:T(8,128)(2,1)}) custom-call(bf16[160,2304]{1,0:T(8,128)(2,1)} %get-tuple-element.103.own, bf16[1152,2304]{1,0:T(8,128)(2,1)} %w_gate.3, bf16[1152,2304]{1,0:T(8,128)(2,1)} %w_up.3, ...), custom_call_target="tpu_custom_call" | custom-call | flops 20384317440 | bytes 24772608 | tf_op jit(solution)/shard_map/pallas_call | solution.py:482
  310.7 0.0 all-gather.11.cloned.1.call-update
  310.7 0.0 all-gather.9.cloned.1.call-start
  310.8 0.6 reshape.159.lower
  311.4 0.6 reshape.157.gain_out
  312.0 0.6 reshape.156.gain_in
  312.6 0.8 reduce.log_total
  313.4 0.0 all-gather.9.cloned.1.call-update
  313.5 0.0 reduce-scatter.5.cloned.1.call-start
  313.5 133.0 %shard_map.240 = (f32[160,2304]{1,0:T(8,128)}, f32[2,2304]{1,0:T(2,128)}, bf16[640,1024]{1,0:T(8,128)(2,1)}, bf16[2304,2048]{1,0:T(8,128)(2,1)}, bf16[2304,1024]...) custom-call(f32[160,2304]{1,0:T(8,128)} %get-tuple-element.61.grad_model, f32[160,2304]{1,0:T(8,128)} %copy-done.1, ...), custom_call_target="tpu_custom_call" | custom-call | flops 217432719360 | tf_op jit(solution)/shard_map/pallas_call | solution.py:1332
  446.6 0.0 copy-start.9
  446.6 0.0 reduce-scatter.5.cloned.1.call-update
  446.6 0.0 reduce-scatter.3.cloned.1.call-start
  446.7 0.6 copy-done.9
  447.3 0.6 reshape.170
  447.9 0.6 fusion.7
  448.5 0.0 reduce-scatter.3.cloned.1.call-update
  448.5 0.0 all-gather.11.cloned.1.call-done.refs_5_
  448.6 0.0 all-gather.9.cloned.1.call-done.refs_3_
  448.6 0.0 copy-start.12
  448.6 0.0 copy-start.13
  448.6 0.0 copy-start.14
  448.6 159.9 %shard_map.241 = (bf16[36,32,2304]{2,1,0:T(8,128)(2,1)}, f32[160,2304]{1,0:T(8,128)}, f32[1,2304]{1,0:T(1,128)}) custom-call(bf16[1280,1152]{1,0:T(8,128)(2,1)} %bitcast.34, bf16[1280,2304]{1,0:T(8,128)(2,1)} %bitcast.28, bf16[4,160,1024]{2,1,0:T(8,128)(2,1)} %bitcast.36, bf16[2304,2048]{1,0:T(8,128)(2,1)} %all-gather.9.cloned.1.call-done.refs_3_, ...), custom_call_target="tpu_custom_call" | custom-call | flops 217432719360 | tf_op jit(solution)/shard_map/pallas_call | solution.py:1613
  608.5 0.0 reduce-scatter.5.cloned.1.call-done.refs_3_
  608.5 0.0 reduce-scatter.3.cloned.1.call-done
  608.6 1.4 pad_maximum_fusion.refs_4_
  609.9 201.1 %shard_map.242 = (bf16[3,96,2048]{2,1,0:T(8,128)(2,1)}, bf16[36,32,2304]{2,1,0:T(8,128)(2,1)}, bf16[288,4096]{1,0:T(8,128)(2,1)}, f32[4,2304]{1,0:T(4,128)}) custom-call(bf16[1280,1152]{1,0:T(8,128)(2,1)} %bitcast.32, bf16[1280,2304]{1,0:T(8,128)(2,1)} %bitcast.29, bf16[3,96,2048]{2,1,0:T(8,128)(2,1)} %bitcast.27, ...), custom_call_target="tpu_custom_call" | custom-call | flops 217432719360 | tf_op jit(solution)/shard_map/pallas_call | solution.py:1613
  811.0 0.0 slice-start.4
  811.0 3.1 slice.36
  814.1 1.7 fusion.6
  815.8 0.7 slice_reduce_fusion
  816.5 0.0 copy-done.6
  816.5 1.8 bitcast_convert_fusion
  818.3 0.0 slice-done.5
  818.3 0.0 slice-start
  818.3 5.5 bitcast_convert_fusion.1
  823.8 4.9 convert_element_type.41
  828.7 4.9 convert_element_type.43
  833.7 1.1 copy.29
  (49 shorter events, 0.1 us)
Async XLA Ops:
  7.2 1.6 copy-start.19
  7.2 1.7 copy-start.18
  7.2 3.2 copy-start.17
  7.2 3.2 copy-start.10
  7.2 3.2 copy-start.11
  7.2 116.5 %all-gather.5.cloned.1.call-start = ((), (), s32[]{:S(2)}) async-start(), calls=%async_computation.2 | async-start | bytes 10616832 | tf_op jit(solution)/shard_map/all_gather | solution.py:94
  8.0 125.6 %all-gather.7.cloned.1.call-start = ((), (), s32[]{:S(2)}) async-start(), calls=%async_computation.3 | async-start | bytes 5308416 | tf_op jit(solution)/shard_map/all_gather | solution.py:94
  8.7 439.8 %all-gather.11.cloned.1.call-start = ((), (), s32[]{:S(2)}) async-start(), calls=%async_computation.5 | async-start | bytes 5308416 | tf_op jit(solution)/shard_map/all_gather | solution.py:94
  123.7 7.4 copy-start.7
  131.1 1.1 copy-start.3
  132.3 81.1 %copy-start.1 = (f32[160,2304]{1,0:T(8,128)}, f32[160,2304]{1,0:T(8,128)S(1)}, u32[]{:S(2)}) copy-start(f32[160,2304]{1,0:T(8,128)S(1)} %get-tuple-element.100.mid) | copy-start | bytes 4423684
  133.6 78.4 %copy-start.4 = (bf16[160,2304]{1,0:T(8,128)(2,1)S(1)}, bf16[160,2304]{1,0:T(8,128)(2,1)}, u32[]{:S(2)}) copy-start(bf16[160,2304]{1,0:T(8,128)(2,1)} %cotangent.1) | copy-start | bytes 2211844
  210.2 1.8 copy-start
  215.6 97.0 %copy-start.8 = (f32[2,640,1]{2,1,0:T(8,128)S(1)}, f32[2,640,1]{2,1,0:T(8,128)}, u32[]{:S(2)}) copy-start(f32[2,640,1]{2,1,0:T(8,128)} %get-tuple-element.64) | copy-start | bytes 15364
  310.7 137.8 %all-gather.9.cloned.1.call-start = ((), (), s32[]{:S(2)}) async-start(), calls=%async_computation.4 | async-start | bytes 10616832 | tf_op jit(solution)/shard_map/all_gather | solution.py:94
  313.5 295.0 %reduce-scatter.5.cloned.1.call-start = ((), (), s32[]{:S(2)}) async-start(), calls=%async_computation.7 | async-start | bytes 5308416 | tf_op jit(solution)/shard_map/reduce_scatter | solution.py:98
  446.6 0.7 copy-start.9
  446.6 1.3 copy-start.16
  446.6 161.9 %reduce-scatter.3.cloned.1.call-start = ((), (), s32[]{:S(2)}) async-start(), calls=%async_computation.6 | async-start | bytes 10616832 | tf_op jit(solution)/shard_map/reduce_scatter | solution.py:98
  448.6 160.0 %copy-start.12 = (f32[1,2304]{1,0:T(1,128)S(1)}, f32[1,2304]{1,0:T(1,128)}, u32[]{:S(2)}) copy-start(f32[1,2304]{1,0:T(1,128)} %reshape.170) | copy-start | bytes 27652
  448.6 160.0 %copy-start.13 = (f32[1,2304]{1,0:T(1,128)S(1)}, f32[1,2304]{1,0:T(1,128)}, u32[]{:S(2)}) copy-start(f32[1,2304]{1,0:T(1,128)} %get-tuple-element.105) | copy-start | bytes 27652
  448.6 160.0 %copy-start.14 = (f32[1,2304]{1,0:T(1,128)S(1)}, f32[1,2304]{1,0:T(1,128)}, u32[]{:S(2)}) copy-start(f32[1,2304]{1,0:T(1,128)} %get-tuple-element.106) | copy-start | bytes 27652
  811.0 3.1 copy-start.2
  811.0 7.3 slice-start.4
  814.1 1.7 copy-start.15
  814.1 2.4 copy-start.6
  814.1 4.2 slice-start.5
  816.5 7.3 slice-start.2
  818.3 5.5 slice-start.3
  818.3 10.4 %slice-start = ((s8[5308416]{0:T(1024)(128)(4,1)}), s8[4194304]{0:T(1024)(128)(4,1)S(1)}, s32[]{:S(2)}) async-start(s8[5308416]{0:T(1024)(128)(4,1)} %bitcast.19), calls=%async_computation.8 | async-start | bytes 8388608
  823.8 4.9 slice-start.1
  828.7 4.9 copy-start.5
Sparse Core Ops, SparseCore 0:
  9.9 73.3 all-gather.4
  85.2 44.0 all-gather.6
  310.9 37.0 all-gather.10
  349.7 72.2 all-gather.8
  446.7 53.2 reduce-scatter.4
  503.8 76.4 reduce-scatter.2
